TPU v7x, 32 devices: a whole 2x2x4 slice. The times are simulated.
32 devices in a mesh: parts: 2 (over x), replica: 2 (over core), tensor: 8 (over z, y).
Axes of the slice: x: 2, y: 2, z: 4, core: 2. Of those that a mesh axis runs over, the one named last changes fastest.
Arguments:
- hidden: bfloat16 [256, 8192], P(('parts', 'replica', 'tensor')), parts along dimension 0, may hold values from -6 to 6
- gain: float32 [8192], replicated, may hold values from 0.1 to 1.9
- request_adapter_index: int32 [256], P(('parts', 'replica', 'tensor')), parts along dimension 0, may hold values from 0 to 63
- lengths: int32 [256], P(('parts', 'replica', 'tensor')), parts along dimension 0, may hold values from 1 to 128, as said below
- rotated_key_cache: bfloat16 [256, 1, 128, 128], P(('parts', 'replica', 'tensor')), parts along dimension 0, may hold values from -160 to 160
- earlier_value_cache: bfloat16 [256, 1, 128, 128], P(('parts', 'replica', 'tensor')), parts along dimension 0, may hold values from -6 to 6
- query_weight: bfloat16 [8192, 1024], P(None, 'tensor'), may hold values from -0.0625 to 0.0625
- key_value_weight: bfloat16 [8192, 256], P(None, 'tensor'), may hold values from -0.0625 to 0.0625
- output_weight: bfloat16 [1024, 8192], P('tensor'), may hold values from -0.1875 to 0.1875
- down_weight_qkv: bfloat16 [8192, 64, 192], P('tensor', 'replica'), may hold values from -0.0625 to 0.0625
- up_weight_query: bfloat16 [64, 64, 1024], P(None, 'replica', 'tensor'), may hold values from -0.75 to 0.75
- up_weight_key_value: bfloat16 [64, 64, 256], P(None, 'replica', 'tensor'), may hold values from -0.75 to 0.75
- down_weight_output: bfloat16 [1024, 64, 64], P('tensor', 'replica'), may hold values from -0.1875 to 0.1875
- up_weight_output: bfloat16 [64, 64, 8192], P(None, 'replica', 'tensor'), may hold values from -0.75 to 0.75
Outputs:
- attn_out: bfloat16 [256, 8192], P(('parts', 'replica', 'tensor')), parts along dimension 0
There are 2 independent parts, one for each index of `parts`. A program takes and returns all parts, laid end to end along the dimension named above; an argument that names none is the same for every part. Nothing has to cross between parts.
Inputs may be any that keep to these rules, and one draw needn't show every extreme that they name: `lengths`: some request of every draw has 128 cached positions.
All inputs are finite; a program needn't handle non-finite values.
Results may differ from a plain program's by a relative error of at most 0.015.
The roundings to bfloat16 on the way count: a program that leaves them out, or rounds other values in their place, can miss the bound.
Values may be sent and summed in bfloat16 or wider, within the bound.
A program may use at most 128 MiB of HBM per device.

v0:
```python
import jax
import jax.numpy as jnp
from jax import lax
from jax.sharding import PartitionSpec as P

HEAD_WIDTH = 128


EPSILON = 1e-05


def rotate(heads_in, positions):
    half_dim = HEAD_WIDTH // 2
    frequency = 10000.0 ** (-jnp.arange(half_dim, dtype=jnp.float32) * 2.0 / HEAD_WIDTH)
    angles = positions.astype(jnp.float32)[:, None] * frequency[None, :]
    cosine = jnp.cos(angles)[:, None, :]
    sine_part = jnp.sin(angles)[:, None, :]
    first_half = heads_in[..., :half_dim]
    second_half = heads_in[..., half_dim:]
    return jnp.concatenate(
        [
            first_half * cosine - second_half * sine_part,
            second_half * cosine + first_half * sine_part,
        ],
        -1,
    )


def pick(left_rows, table, onehot):
    inner_dim, slots, columns = table.shape
    product = jnp.dot(
        left_rows, table.reshape(inner_dim, slots * columns), preferred_element_type=jnp.float32
    )
    product = product.reshape(left_rows.shape[0], slots, columns)
    return jnp.sum(product * onehot[:, :, None], axis=1)


def attend(q_rot, k_rot, fresh_values, rotated_key_cache, earlier_value_cache, lengths):
    score_scale = HEAD_WIDTH ** (-0.5)
    scores = (
        jnp.einsum("rgjd,rgld->rgjl", q_rot, rotated_key_cache, preferred_element_type=jnp.float32)
        * score_scale
    )
    cached = rotated_key_cache.shape[2]
    visible = (jnp.arange(cached, dtype=jnp.int32)[None, :] < lengths[:, None])[:, None, None, :]
    scores = jnp.where(visible, scores, -jnp.inf)
    score_new = (
        jnp.einsum("rgjd,rgd->rgj", q_rot, k_rot, preferred_element_type=jnp.float32) * score_scale
    )
    highest = jnp.maximum(jnp.max(scores, axis=-1), score_new)
    weights_cache = jnp.exp(scores - highest[..., None])
    weight_new = jnp.exp(score_new - highest)
    denominator = jnp.sum(weights_cache, axis=-1) + weight_new
    weights_cache = (weights_cache / denominator[..., None]).astype(jnp.bfloat16)
    weight_new = (weight_new / denominator).astype(jnp.bfloat16)
    mixed = jnp.einsum(
        "rgjl,rgld->rgjd", weights_cache, earlier_value_cache, preferred_element_type=jnp.float32
    )
    mixed = (
        mixed
        + weight_new.astype(jnp.float32)[..., None]
        * fresh_values.astype(jnp.float32)[:, :, None, :]
    )
    return mixed.astype(jnp.bfloat16).reshape(q_rot.shape[0], -1)


def shards(
    hidden,
    gain,
    request_adapter_index,
    lengths,
    rotated_key_cache,
    earlier_value_cache,
    query_weight,
    key_value_weight,
    output_weight,
    down_weight_qkv,
    up_weight_query,
    up_weight_key_value,
    down_weight_output,
    up_weight_output,
):
    tensor_at = lax.axis_index("tensor")
    tensor_size = lax.axis_size("tensor")
    replica_at = lax.axis_index("replica")
    hidden_wide = hidden.astype(jnp.float32)
    mean_square = jnp.mean(hidden_wide * hidden_wide, axis=-1, keepdims=True)
    normalized_input = (hidden_wide * lax.rsqrt(mean_square + EPSILON) * gain).astype(jnp.bfloat16)
    gathered = lax.all_gather(normalized_input, "tensor", axis=0, tiled=True)
    every_id = lax.all_gather(request_adapter_index, ("replica", "tensor"), axis=0, tiled=True)
    batch_rows = gathered.shape[0]
    own_ids = lax.dynamic_slice_in_dim(every_id, replica_at * batch_rows, batch_rows)
    local_input = down_weight_qkv.shape[0]
    features = lax.dynamic_slice_in_dim(gathered, tensor_at * local_input, local_input, 1)
    base_query = jnp.dot(gathered, query_weight, preferred_element_type=jnp.float32)
    base_kv = jnp.dot(gathered, key_value_weight, preferred_element_type=jnp.float32)
    table_a, table_bq, table_bkv, table_ao, table_bo = (
        lax.all_gather(down_weight_qkv, "replica", axis=1, tiled=True),
        lax.all_gather(up_weight_query, "replica", axis=1, tiled=True),
        lax.all_gather(up_weight_key_value, "replica", axis=1, tiled=True),
        lax.all_gather(down_weight_output, "replica", axis=1, tiled=True),
        lax.all_gather(up_weight_output, "replica", axis=1, tiled=True),
    )
    slots = table_a.shape[1]
    onehot = (own_ids[:, None] == jnp.arange(slots, dtype=jnp.int32)[None, :]).astype(jnp.float32)
    reduced_input = lax.psum(pick(features, table_a, onehot), "tensor").astype(jnp.bfloat16)
    rank_size = table_bq.shape[0]
    reduced_query = reduced_input[:, :rank_size]
    shrink_kv = jnp.where(
        tensor_at < tensor_size // 2,
        reduced_input[:, rank_size : 2 * rank_size],
        reduced_input[:, 2 * rank_size :],
    )
    delta_qkv = jnp.concatenate(
        [pick(reduced_query, table_bq, onehot), pick(shrink_kv, table_bkv, onehot)], 1
    )
    query_cols = query_weight.shape[1]
    query_part = (base_query + delta_qkv[:, :query_cols]).astype(jnp.bfloat16)
    kv_part = (base_kv + delta_qkv[:, query_cols:]).astype(jnp.bfloat16)
    query_rows, kv_rows = (
        lax.all_to_all(query_part, "tensor", split_axis=0, concat_axis=1, tiled=True),
        lax.all_to_all(kv_part, "tensor", split_axis=0, concat_axis=1, tiled=True),
    )
    own_rows = hidden.shape[0]
    head_count = query_rows.shape[1] // HEAD_WIDTH
    kv_heads = kv_rows.shape[1] // (2 * HEAD_WIDTH)
    group_size = head_count // kv_heads
    q_rot = rotate(
        query_rows.reshape(own_rows, head_count, HEAD_WIDTH).astype(jnp.float32), lengths
    ).astype(jnp.bfloat16)
    q_rot = q_rot.reshape(own_rows, kv_heads, group_size, HEAD_WIDTH)
    k_rot = rotate(
        kv_rows[:, : kv_heads * HEAD_WIDTH]
        .reshape(own_rows, kv_heads, HEAD_WIDTH)
        .astype(jnp.float32),
        lengths,
    ).astype(jnp.bfloat16)
    fresh_values = kv_rows[:, kv_heads * HEAD_WIDTH :].reshape(own_rows, kv_heads, HEAD_WIDTH)
    attention_mixed = attend(
        q_rot, k_rot, fresh_values, rotated_key_cache, earlier_value_cache, lengths
    )
    heads_part = lax.all_to_all(attention_mixed, "tensor", split_axis=1, concat_axis=0, tiled=True)
    reduced_output = lax.psum(pick(heads_part, table_ao, onehot), "tensor").astype(jnp.bfloat16)
    delta_out = pick(reduced_output, table_bo, onehot)
    out_cols = delta_out.shape[1]
    full_term = jnp.dot(heads_part, output_weight, preferred_element_type=jnp.float32)
    column_block = lax.dynamic_slice_in_dim(full_term, tensor_at * out_cols, out_cols, 1)
    summed = lax.psum_scatter(
        lax.dynamic_update_slice_in_dim(
            full_term, column_block + delta_out, tensor_at * out_cols, 1
        ),
        "tensor",
        scatter_dimension=0,
        tiled=True,
    )
    return summed.astype(jnp.bfloat16)


def solution(mesh):
    return jax.shard_map(
        shards,
        mesh=mesh,
        in_specs=(
            P(("parts", "replica", "tensor"), None),
            P(),
            P(("parts", "replica", "tensor")),
            P(("parts", "replica", "tensor")),
            P(("parts", "replica", "tensor"), None, None, None),
            P(("parts", "replica", "tensor"), None, None, None),
            P(None, "tensor"),
            P(None, "tensor"),
            P("tensor", None),
            P("tensor", "replica", None),
            P(None, "replica", "tensor"),
            P(None, "replica", "tensor"),
            P("tensor", "replica", None),
            P(None, "replica", "tensor"),
        ),
        out_specs=P(("parts", "replica", "tensor"), None),
        check_vma=False,
    )
```

profile of v0, /device:TPU:0, one launch (start us, length us, event | category | flops | bytes accessed | tf_op | source)
XLA Modules:
  0.0 309.7 jit_solution(4760959605941195745)
XLA Ops:
  7.8 1.7 fusion.18
  13.7 13.9 %all-reduce = s32[128]{0:T(128)S(1)} all-reduce(s32[128]{0:T(128)S(1)} %dynamic-update-slice), channel_id=1, replica_groups=mesh['parts'=2,'replica'=2,'tensor'=8] {'replica','tensor'}, use_global_device_ids=true, to_apply=%add | all-reduce | flops 128 | bytes 1024
  27.7 2.3 all_gather.25
  30.2 22.3 %all-gather.6.cloned.1.call-done = bf16[64,8192]{1,0:T(8,128)(2,1)} async-done(((bf16[8,8192]{1,0:T(8,128)(2,1)}), bf16[64,8192]{1,0:T(8,128)(2,1)}) %all-gather.6.cloned.1.call-update) | async-done | bytes 1048592 | tf_op jit(solution)/shard_map/all_gather | solution.py:89
  52.5 40.6 %all-gather.8.cloned.1.call-done = bf16[1024,64,192]{0,2,1:T(8,128)(2,1)} async-done(((bf16[1024,32,192]{0,2,1:T(8,128)(2,1)}), bf16[1024,64,192]{0,2,1:T(8,128)(2,1)}) %all-gather.8.cloned.1.call-update) | async-done | bytes 25165840 | tf_op jit(solution)/shard_map/all_gather | solution.py:98
  93.1 12.8 %multiply_reduce_fusion.1 = f32[64,192]{1,0:T(8,128)S(1)} fusion(f32[64,64]{0,1:T(8,128)S(1)} %fusion.23, bf16[1024,64,192]{0,2,1:T(8,128)(2,1)} %all-gather.8.cloned.1.call-done, bf16[64,8192]{1,0:T(8,128)(2,1)} %all-gather.6.cloned.1.call-done, s32[]{:T(128)S(6)} %select_n.21), kind=kOutput, calls=%fused_computation.5 | convolution fusion | flops 1612173312 | bytes 25362436 | tf_op jit(solution)/shard_map/dot_general | solution.py:31
  105.9 37.8 %psum.14 = bf16[64,192]{1,0:T(8,128)(2,1)S(1)} all-reduce(f32[64,192]{1,0:T(8,128)S(1)} %multiply_reduce_fusion.1), channel_id=1, replica_groups=mesh['parts'=2,'replica'=2,'tensor'=8] {'tensor'}, use_global_device_ids=true, to_apply=%region_2.0 | all-reduce | flops 12288 | bytes 73728 | tf_op jit(solution)/shard_map/psum | solution.py:106
  143.7 1.5 fusion.6
  145.2 1.4 fusion.11
  147.4 3.3 %all-to-all-start.1 = ((bf16[8,2,128]{2,1,0:T(2,128)(2,1)}), bf16[8,2,128]{2,1,0:T(2,128)(2,1)S(1)}, u32[]{:S(2)}, u32[]{:S(2)}) async-start(bf16[8,2,128]{2,1,0:T(2,128)(2,1)} %reshape.288), calls=%async_computation.1 | async-start | bytes 8192 | tf_op jit(solution)/shard_map/all_to_all | solution.py:122
  150.8 2.2 multiply_reduce_fusion.3
  152.9 2.7 fusion.10
  155.6 1.5 all-to-all-done.1
  157.1 4.4 %all-to-all-start = ((bf16[8,8,128]{2,1,0:T(8,128)(2,1)}), bf16[8,8,128]{2,1,0:T(8,128)(2,1)S(1)}, u32[]{:S(2)}, u32[]{:S(2)}) async-start(bf16[8,8,128]{2,1,0:T(8,128)(2,1)} %fusion.10), calls=%async_computation | async-start | bytes 32768 | tf_op jit(solution)/shard_map/all_to_all | solution.py:121
  161.9 6.2 %all-to-all-done = bf16[8,8,128]{2,1,0:T(8,128)(2,1)S(1)} async-done(((bf16[8,8,128]{2,1,0:T(8,128)(2,1)}), bf16[8,8,128]{2,1,0:T(8,128)(2,1)S(1)}, u32[]{:S(2)}, u32[]{:S(2)}) %all-to-all-start) | async-done | bytes 16416 | tf_op jit(solution)/shard_map/all_to_all | solution.py:121
  170.8 3.3 %all-to-all-start.2 = ((bf16[8,8,128]{2,0,1:T(8,128)(2,1)}), bf16[8,8,128]{2,0,1:T(8,128)(2,1)S(1)}, u32[]{:S(2)}, u32[]{:S(2)}) async-start(bf16[8,8,128]{2,0,1:T(8,128)(2,1)} %copy.30), calls=%async_computation.2 | async-start | bytes 32768 | tf_op jit(solution)/shard_map/all_to_all | solution.py:142
  174.2 6.4 %all-to-all-done.2 = bf16[8,8,128]{2,0,1:T(8,128)(2,1)S(1)} async-done(((bf16[8,8,128]{2,0,1:T(8,128)(2,1)}), bf16[8,8,128]{2,0,1:T(8,128)(2,1)S(1)}, u32[]{:S(2)}, u32[]{:S(2)}) %all-to-all-start.2) | async-done | bytes 16416 | tf_op jit(solution)/shard_map/all_to_all | solution.py:142
  180.6 2.4 multiply_reduce_fusion.2
  183.0 33.5 %psum.15 = bf16[64,64]{1,0:T(8,128)(2,1)S(1)} all-reduce(f32[64,64]{1,0:T(8,128)S(1)} %multiply_reduce_fusion.2), channel_id=1, replica_groups=mesh['parts'=2,'replica'=2,'tensor'=8] {'tensor'}, use_global_device_ids=true, to_apply=%region_8.9 | all-reduce | flops 4096 | bytes 24576 | tf_op jit(solution)/shard_map/psum | solution.py:143
  216.5 16.1 %multiply_reduce_fusion = f32[64,1024]{1,0:T(8,128)S(1)} fusion(f32[64,64]{0,1:T(8,128)S(1)} %fusion.23, bf16[64,64]{1,0:T(8,128)(2,1)S(1)} %psum.15, bf16[8,8,64,1024]{3,2,1,0:T(8,128)(2,1)} %bitcast.104), kind=kOutput, calls=%fused_computation.2 | convolution fusion | flops 545193984 | bytes 8675328 | tf_op jit(solution)/shard_map/dot_general | solution.py:31
  232.6 1.8 fusion.30
  234.4 1.7 add_dynamic-update-slice_fusion
  236.1 65.1 %reduce-scatter.2.cloned.1.call-done = f32[8,8192]{1,0:T(8,128)} async-done(((f32[64,8192]{1,0:T(8,128)}), f32[8,8192]{1,0:T(8,128)}) %reduce-scatter.2.cloned.1.call-update) | async-done | bytes 262160 | tf_op jit(solution)/shard_map/reduce_scatter | solution.py:148
  301.2 1.6 convert_element_type.89
  (57 shorter events, 8.9 us)
Async XLA Ops:
  6.5 226.1 %copy-start = (bf16[128,8192]{1,0:T(8,128)(2,1)S(1)}, bf16[128,8192]{1,0:T(8,128)(2,1)}, u32[]{:S(2)}) copy-start(bf16[128,8192]{1,0:T(8,128)(2,1)} %param.22) | copy-start | bytes 6291460
  6.5 45.9 %all-gather.6.cloned.1.call-start = ((), (), s32[]{:S(2)}) async-start(), calls=%async_computation.4 | async-start | bytes 1179648 | tf_op jit(solution)/shard_map/all_gather | solution.py:89
  9.5 83.6 %all-gather.8.cloned.1.call-start = ((), (), s32[]{:S(2)}) async-start(), calls=%async_computation.5 | async-start | bytes 37748736 | tf_op jit(solution)/shard_map/all_gather | solution.py:98
  10.2 2.0 copy-start.5
  10.2 2.0 copy-start.6
  10.2 3.2 %copy-start.4 = (s32[8]{0:T(128)S(1)}, s32[8]{0:T(128)}, u32[]{:S(2)}) copy-start(s32[8]{0:T(128)} %param.16) | copy-start | bytes 100
  10.3 17.5 %copy-start.2 = (bf16[64,32,32]{0,2,1:T(8,128)(2,1)S(1)}, bf16[64,32,32]{0,2,1:T(8,128)(2,1)}, u32[]{:S(2)}) copy-start(bf16[64,32,32]{0,2,1:T(8,128)(2,1)} %param.25) | copy-start | bytes 393220
  10.3 140.5 %all-gather.10.cloned.1.call-start = ((), (), s32[]{:S(2)}) async-start(), calls=%async_computation.6 | async-start | bytes 1572864 | tf_op jit(solution)/shard_map/all_gather | solution.py:99
  11.0 163.2 %all-gather.12.cloned.1.call-start = ((), (), s32[]{:S(2)}) async-start(), calls=%async_computation.7 | async-start | bytes 1572864 | tf_op jit(solution)/shard_map/all_gather | solution.py:101
  11.6 204.9 %all-gather.14.cloned.1.call-start = ((), (), s32[]{:S(2)}) async-start(), calls=%async_computation.8 | async-start | bytes 12582912 | tf_op jit(solution)/shard_map/all_gather | solution.py:102
  52.5 92.7 %copy-start.1 = (bf16[64,8192]{1,0:T(8,128)(2,1)S(1)}, bf16[64,8192]{1,0:T(8,128)(2,1)}, u32[]{:S(2)}) copy-start(bf16[64,8192]{1,0:T(8,128)(2,1)} %all-gather.6.cloned.1.call-done) | copy-start | bytes 3145732
  143.7 24.7 %copy-start.3 = (bf16[8,1,128,128]{3,2,1,0:T(8,128)(2,1)S(1)}, bf16[8,1,128,128]{3,2,1,0:T(8,128)(2,1)}, u32[]{:S(2)}) copy-start(bf16[8,1,128,128]{3,2,1,0:T(8,128)(2,1)} %param.18) | copy-start | bytes 786436
  147.4 9.7 %all-to-all-start.1 = ((bf16[8,2,128]{2,1,0:T(2,128)(2,1)}), bf16[8,2,128]{2,1,0:T(2,128)(2,1)S(1)}, u32[]{:S(2)}, u32[]{:S(2)}) async-start(bf16[8,2,128]{2,1,0:T(2,128)(2,1)} %reshape.288), calls=%async_computation.1 | async-start | bytes 8192 | tf_op jit(solution)/shard_map/all_to_all | solution.py:122
  157.1 11.0 %all-to-all-start = ((bf16[8,8,128]{2,1,0:T(8,128)(2,1)}), bf16[8,8,128]{2,1,0:T(8,128)(2,1)S(1)}, u32[]{:S(2)}, u32[]{:S(2)}) async-start(bf16[8,8,128]{2,1,0:T(8,128)(2,1)} %fusion.10), calls=%async_computation | async-start | bytes 32768 | tf_op jit(solution)/shard_map/all_to_all | solution.py:121
  170.8 9.9 %all-to-all-start.2 = ((bf16[8,8,128]{2,0,1:T(8,128)(2,1)}), bf16[8,8,128]{2,0,1:T(8,128)(2,1)S(1)}, u32[]{:S(2)}, u32[]{:S(2)}) async-start(bf16[8,8,128]{2,0,1:T(8,128)(2,1)} %copy.30), calls=%async_computation.2 | async-start | bytes 32768 | tf_op jit(solution)/shard_map/all_to_all | solution.py:142
  174.1 127.1 %reduce-scatter.2.cloned.1.call-start = ((), (), s32[]{:S(2)}) async-start(), calls=%async_computation.9 | async-start | bytes 2359296 | tf_op jit(solution)/shard_map/reduce_scatter | solution.py:148
Sparse Core Ops, SparseCore 0:
  9.6 42.8 all-gather.5
  54.0 39.0 all-gather.7
  94.7 10.1 all-gather.9
  106.3 10.1 all-gather.11
  117.9 21.0 all-gather.13
  236.2 64.9 reduce-scatter.1
where the time goes:
time: 310 us
  waiting for transfers between devices  145 us (47%)
  blocking collectives  87.5 us (28%)
  matrix products  42.5 us (14%)
  between operations  14.3 us (5%)
  starting transfers between devices  11.2 us (4%)
  other arithmetic  6.9 us (2%)
    reduce_scatter x1, waiting for transfers between devices, shards(): lax.psum_scatter(lax.dynamic_update_slice_in_dim(full_term, column_block...  65.1 us
    all_gather x1, waiting for transfers between devices, shards(): lax.all_gather(down_weight_qkv, 'replica', axis=1, tiled=True)  40.6 us
    psum x1, blocking collectives, shards(): lax.psum(pick(features, table_a, onehot), 'tensor').astype(jnp.bfloat16)  37.8 us
    dot_general x5, matrix products, pick(): jnp.dot(left_rows, table.reshape(inner_dim, slots * columns), preferred_e...  34.9 us
    psum x1, blocking collectives, shards(): lax.psum(pick(heads_part, table_ao, onehot), 'tensor').astype(jnp.bfloat16)  33.5 us
    all_gather x1, waiting for transfers between devices, shards(): gathered = lax.all_gather(normalized_input, 'tensor', axis=0, tiled=True)  22.3 us
    unnamed x1, blocking collectives  13.9 us
    all_to_all x1, waiting for transfers between devices, shards(): lax.all_to_all(attention_mixed, 'tensor', split_axis=1, concat_axis=0, ti...  6.44 us
  transfers between devices with their start and end apart: 9, of which 6 were waited for; matrix products, arithmetic and copies ran while one was open for 9% of the time, Pallas kernels for 0%

commit v1 on v0

v1 whole, which is shorter than its diff:
```python
import functools

import jax
import jax.numpy as jnp
from jax import lax
from jax.experimental import pallas as pl
from jax.experimental.pallas import tpu as pltpu
from jax.sharding import PartitionSpec as P

HEAD_WIDTH = 128
EPSILON = 1e-05
MESH = pl.DeviceIdType.MESH
VMEM_LIMIT = 48 * 1024 * 1024


def rotate(heads_in, positions):
    half_dim = HEAD_WIDTH // 2
    frequency = 10000.0 ** (-jnp.arange(half_dim, dtype=jnp.float32) * 2.0 / HEAD_WIDTH)
    angles = positions.astype(jnp.float32)[:, None] * frequency[None, :]
    cosine = jnp.cos(angles)[:, None, :]
    sine_part = jnp.sin(angles)[:, None, :]
    first_half = heads_in[..., :half_dim]
    second_half = heads_in[..., half_dim:]
    return jnp.concatenate(
        [
            first_half * cosine - second_half * sine_part,
            second_half * cosine + first_half * sine_part,
        ],
        -1,
    )


def pick_down(left_rows, table, onehot):
    inner_dim, slots, columns = table.shape
    product = jnp.dot(
        left_rows, table.reshape(inner_dim, slots * columns), preferred_element_type=jnp.float32
    )
    product = product.reshape(left_rows.shape[0], slots, columns)
    return jnp.sum(product * onehot[:, :, None], axis=1)


def pick_up(left_rows, table, onehot):
    rank, slots, columns = table.shape
    spread = left_rows[:, :, None] * onehot.astype(left_rows.dtype)[:, None, :]
    return jnp.dot(
        spread.reshape(left_rows.shape[0], rank * slots),
        table.reshape(rank * slots, columns),
        preferred_element_type=jnp.float32,
    )


def attend(q_rot, k_rot, fresh_values, rotated_key_cache, earlier_value_cache, lengths):
    score_scale = HEAD_WIDTH ** (-0.5)
    scores = (
        jnp.einsum("rgjd,rgld->rgjl", q_rot, rotated_key_cache, preferred_element_type=jnp.float32)
        * score_scale
    )
    cached = rotated_key_cache.shape[2]
    visible = (jnp.arange(cached, dtype=jnp.int32)[None, :] < lengths[:, None])[:, None, None, :]
    scores = jnp.where(visible, scores, -jnp.inf)
    score_new = (
        jnp.einsum("rgjd,rgd->rgj", q_rot, k_rot, preferred_element_type=jnp.float32) * score_scale
    )
    highest = jnp.maximum(jnp.max(scores, axis=-1), score_new)
    weights_cache = jnp.exp(scores - highest[..., None])
    weight_new = jnp.exp(score_new - highest)
    denominator = jnp.sum(weights_cache, axis=-1) + weight_new
    weights_cache = (weights_cache / denominator[..., None]).astype(jnp.bfloat16)
    weight_new = (weight_new / denominator).astype(jnp.bfloat16)
    mixed = jnp.einsum(
        "rgjl,rgld->rgjd", weights_cache, earlier_value_cache, preferred_element_type=jnp.float32
    )
    mixed = (
        mixed
        + weight_new.astype(jnp.float32)[..., None]
        * fresh_values.astype(jnp.float32)[:, :, None, :]
    )
    return mixed.astype(jnp.bfloat16).reshape(q_rot.shape[0], -1)


def where_am_i():
    return lax.axis_index("parts"), lax.axis_index("replica"), lax.axis_index("tensor")


def greet(peers):
    barrier = pltpu.get_barrier_semaphore()
    for peer in peers:
        pl.semaphore_signal(barrier, inc=1, device_id=peer, device_id_type=MESH)
    pl.semaphore_wait(barrier, len(peers))


def all_peers(tensor_size):
    part, replica, tensor = where_am_i()
    total = 2 * tensor_size
    me = replica * tensor_size + tensor
    found = []
    for step in range(1, total):
        other = lax.rem(me + step, total)
        found.append((other, (part, other // tensor_size, lax.rem(other, tensor_size))))
    return me, found


def tensor_peers(tensor_size):
    part, replica, tensor = where_am_i()
    found = []
    for step in range(1, tensor_size):
        other = lax.rem(tensor + step, tensor_size)
        found.append((other, (part, replica, other)))
    return tensor, found


def remote(src, dst, send, recv, peer):
    return pltpu.make_async_remote_copy(
        src_ref=src, dst_ref=dst, send_sem=send, recv_sem=recv, device_id=peer, device_id_type=MESH
    )


def exchange_kernel(tensor_size, x_ref, y_ref, send_sem, recv_sem):
    me, peers = all_peers(tensor_size)
    greet([peer for _, peer in peers])
    copies = []
    for step, (other, peer) in enumerate(peers):
        copy = remote(x_ref.at[other], y_ref.at[me], send_sem.at[step], recv_sem.at[step], peer)
        copy.start()
        copies.append(copy)
    y_ref[me] = x_ref[me]
    for copy in copies:
        copy.wait()


def call(kernel, outs, scratch, collective_id, *operands):
    return pl.pallas_call(
        kernel,
        out_shape=outs,
        in_specs=[pl.BlockSpec(memory_space=pltpu.VMEM)] * len(operands),
        out_specs=jax.tree.map(lambda _: pl.BlockSpec(memory_space=pltpu.VMEM), outs),
        scratch_shapes=scratch,
        compiler_params=pltpu.CompilerParams(
            collective_id=collective_id, has_side_effects=True, vmem_limit_bytes=VMEM_LIMIT
        ),
    )(*operands)


def exchange(x, tensor_size, collective_id):
    count = 2 * tensor_size - 1
    return call(
        functools.partial(exchange_kernel, tensor_size),
        jax.ShapeDtypeStruct(x.shape, x.dtype),
        [pltpu.SemaphoreType.DMA((count,)), pltpu.SemaphoreType.DMA((count,))],
        collective_id,
        x,
    )


def reduce_kernel(tensor_size, x_ref, y_ref, land, mine, send_a, recv_a, send_b, recv_b):
    me, peers = tensor_peers(tensor_size)
    greet([peer for _, peer in peers])
    copies = []
    for step, (other, peer) in enumerate(peers):
        copy = remote(x_ref.at[other], land.at[me], send_a.at[step], recv_a.at[step], peer)
        copy.start()
        copies.append(copy)
    land[me] = x_ref[me]
    for copy in copies:
        copy.wait()
    total = land[0]
    for step in range(1, tensor_size):
        total = total + land[step]
    mine[...] = total.astype(mine.dtype)
    copies = []
    for step, (other, peer) in enumerate(peers):
        copy = remote(mine, y_ref.at[me], send_b.at[step], recv_b.at[step], peer)
        copy.start()
        copies.append(copy)
    y_ref[me] = mine[...]
    for copy in copies:
        copy.wait()


def reduce_and_gather(x, tensor_size, collective_id):
    rows, width = x.shape
    padded = -(-width // 128) * 128
    blocks = jnp.pad(x, ((0, 0), (0, padded - width))).reshape(
        tensor_size, rows // tensor_size, padded
    )
    count = tensor_size - 1
    done = call(
        functools.partial(reduce_kernel, tensor_size),
        jax.ShapeDtypeStruct(blocks.shape, jnp.bfloat16),
        [pltpu.VMEM(blocks.shape, jnp.float32), pltpu.VMEM(blocks.shape[1:], jnp.bfloat16)]
        + [pltpu.SemaphoreType.DMA((count,))] * 4,
        collective_id,
        blocks,
    )
    return done.reshape(rows, padded)[:, :width]


def gather_kernel(
    tensor_size, x_ref, id_ref, g_ref, fo_ref, ids_ref,
    send_id, recv_id, send_up, recv_up, send_dn, recv_dn, send_y, recv_y, send_f, recv_f,
):
    part, replica, tensor = where_am_i()
    me, peers = all_peers(tensor_size)
    greet([peer for _, peer in peers])
    depth = tensor_size // 2
    level, side = tensor // 2, lax.rem(tensor, 2)
    above = (part, replica, lax.rem(tensor + 2, tensor_size))
    below = (part, replica, lax.rem(tensor + tensor_size - 2, tensor_size))
    across = (part, replica, level * 2 + 1 - side)
    twin = (part, 1 - replica, tensor)

    def block(at):
        return jnp.clip(at, 0, depth - 1) * 2 + side

    def up(step):
        at = block(level - step)
        return remote(g_ref.at[at], g_ref.at[at], send_up.at[step], recv_up.at[step], above)

    def up_in(step):
        at = block(level - step - 1)
        return remote(g_ref.at[at], g_ref.at[at], send_up.at[step], recv_up.at[step], above)

    def down(step):
        at = block(level + step)
        return remote(g_ref.at[at], g_ref.at[at], send_dn.at[step], recv_dn.at[step], below)

    def down_in(step):
        at = block(level + step + 1)
        return remote(g_ref.at[at], g_ref.at[at], send_dn.at[step], recv_dn.at[step], below)

    def cross(at_level):
        at = jnp.clip(at_level, 0, depth - 1)
        return remote(
            g_ref.at[at * 2 + side], g_ref.at[at * 2 + side], send_y.at[at], recv_y.at[at], across
        )

    def cross_in(at):
        return remote(
            g_ref.at[at * 2 + 1 - side], g_ref.at[at * 2 + 1 - side], send_y.at[at], recv_y.at[at], across
        )

    g_ref[tensor] = x_ref[...]
    has_above, has_below = level < depth - 1, level > 0

    @pl.when(has_above)
    def _():
        up(0).start()

    @pl.when(has_below)
    def _():
        down(0).start()

    cross(level).start()
    copies = []
    for step, (other, peer) in enumerate(peers):
        copy = remote(id_ref, ids_ref.at[me], send_id.at[step], recv_id.at[step], peer)
        copy.start()
        copies.append(copy)
    ids_ref[me] = id_ref[...]
    for step in range(depth - 1):

        @pl.when(level - step - 1 >= 0)
        def _():
            up_in(step).wait_recv()
            if step + 1 < depth - 1:

                @pl.when(has_above)
                def _():
                    up(step + 1).start()

            cross(level - step - 1).start()

        @pl.when(level + step + 1 < depth)
        def _():
            down_in(step).wait_recv()
            if step + 1 < depth - 1:

                @pl.when(has_below)
                def _():
                    down(step + 1).start()

            cross(level + step + 1).start()

    for at in range(depth):
        cross_in(at).wait_recv()
    swap = remote(g_ref.at[:, tensor], fo_ref, send_f, recv_f, twin)
    swap.start()
    for step in range(depth - 1):

        @pl.when(jnp.logical_and(has_above, level - step >= 0))
        def _():
            up(step).wait_send()

        @pl.when(jnp.logical_and(has_below, level + step < depth))
        def _():
            down(step).wait_send()

    for at in range(depth):
        cross(at).wait_send()
    for copy in copies:
        copy.wait()
    swap.wait()


def output_kernel(
    tensor_size, x_ref, d_ref, sum_ref, e_ref, land, send_x, recv_x, send_d, recv_d
):
    me, everyone = all_peers(tensor_size)
    tensor, peers = tensor_peers(tensor_size)
    greet([peer for _, peer in everyone])
    copies = []
    for step, (other, peer) in enumerate(peers):
        copy = remote(x_ref.at[other], land.at[tensor], send_x.at[step], recv_x.at[step], peer)
        copy.start()
        copies.append(copy)
    for step, (other, peer) in enumerate(everyone):
        copy = remote(d_ref.at[other], e_ref.at[me], send_d.at[step], recv_d.at[step], peer)
        copy.start()
        copies.append(copy)
    land[tensor] = x_ref[tensor]
    e_ref[me] = d_ref[me]
    for copy in copies:
        copy.wait()
    width = 512

    def column(at, carry):
        spot = pl.ds(pl.multiple_of(at * width, width), width)
        total = land[0, :, spot].astype(jnp.float32)
        for step in range(1, tensor_size):
            total = total + land[step, :, spot].astype(jnp.float32)
        sum_ref[:, spot] = total
        return carry

    lax.fori_loop(0, sum_ref.shape[1] // width, column, 0)


def fold_slices(rows, slices):
    count, width = rows.shape
    part = width // slices // 2
    return rows.reshape(count, slices, 2, part).transpose(1, 0, 2, 3).reshape(slices, 2 * count, part)


def shards(
    hidden,
    gain,
    request_adapter_index,
    lengths,
    rotated_key_cache,
    earlier_value_cache,
    query_weight,
    key_value_weight,
    output_weight,
    down_weight_qkv,
    up_weight_query,
    up_weight_key_value,
    down_weight_output,
    up_weight_output,
):
    tensor_at = lax.axis_index("tensor")
    size = lax.axis_size("tensor")
    replica_at = lax.axis_index("replica")
    own_rows, model_width = hidden.shape
    batch_rows = own_rows * size
    every_row = 2 * batch_rows
    hidden_wide = hidden.astype(jnp.float32)
    mean_square = jnp.mean(hidden_wide * hidden_wide, axis=-1, keepdims=True)
    normalized_input = (hidden_wide * lax.rsqrt(mean_square + EPSILON) * gain).astype(jnp.bfloat16)

    folded = fold_slices(normalized_input, size)
    half = folded.shape[2]
    id_tile = jnp.broadcast_to(request_adapter_index[:, None], (own_rows, 128))
    depth = size // 2
    dma = pltpu.SemaphoreType.DMA
    steps = max(depth - 1, 1)
    gathered, other_features, id_tiles = call(
        functools.partial(gather_kernel, size),
        (
            jax.ShapeDtypeStruct((size,) + folded.shape, jnp.bfloat16),
            jax.ShapeDtypeStruct(folded.shape, jnp.bfloat16),
            jax.ShapeDtypeStruct((2 * size, own_rows, 128), jnp.int32),
        ),
        [dma((2 * size - 1,)), dma((2 * size - 1,))] + [dma((steps,))] * 4 + [dma((depth,))] * 2
        + [dma, dma],
        0,
        folded,
        id_tile,
    )
    own_features = lax.dynamic_index_in_dim(gathered, tensor_at, 1, keepdims=False)

    def unfold(blocks):
        return (
            blocks.reshape(size, own_rows, 2, half).reshape(batch_rows, 2 * half)
        )

    own_features, other_features = unfold(own_features), unfold(other_features)
    features = jnp.where(
        replica_at == 0,
        jnp.concatenate([own_features, other_features], 0),
        jnp.concatenate([other_features, own_features], 0),
    )
    full = (
        gathered.reshape(size, size, own_rows, 2, half)
        .transpose(0, 2, 1, 3, 4)
        .reshape(batch_rows, model_width)
    )
    every_id = id_tiles[:, :, 0].reshape(every_row)
    slots = down_weight_qkv.shape[1]
    onehot = (
        (every_id - replica_at * slots)[:, None] == jnp.arange(slots, dtype=jnp.int32)[None, :]
    ).astype(jnp.float32)
    reduced_input = reduce_and_gather(pick_down(features, down_weight_qkv, onehot), size, 1)
    base = jnp.concatenate(
        [
            jnp.dot(full, query_weight, preferred_element_type=jnp.float32),
            jnp.dot(full, key_value_weight, preferred_element_type=jnp.float32),
        ],
        1,
    )
    rank_size = up_weight_query.shape[0]
    shrink_kv = jnp.where(
        tensor_at < size // 2,
        reduced_input[:, rank_size : 2 * rank_size],
        reduced_input[:, 2 * rank_size :],
    )
    delta = jnp.concatenate(
        [
            pick_up(reduced_input[:, :rank_size], up_weight_query, onehot),
            pick_up(shrink_kv, up_weight_key_value, onehot),
        ],
        1,
    ).reshape(2, batch_rows, -1)
    own = (jnp.arange(2) == replica_at)[:, None, None]
    delta = delta + jnp.where(own, base[None], 0.0)
    query_cols = query_weight.shape[1]
    kv_cols = key_value_weight.shape[1]
    padded = -(-(query_cols + kv_cols) // 128) * 128
    delta = jnp.pad(delta, ((0, 0), (0, 0), (0, padded - query_cols - kv_cols)))
    arrived = exchange(delta.reshape(2 * size, own_rows, padded), size, 2)
    arrived = arrived.reshape(2, size, own_rows, padded)
    arrived = (arrived[0] + arrived[1]).astype(jnp.bfloat16).transpose(1, 0, 2)
    query_rows = arrived[:, :, :query_cols].reshape(own_rows, size * query_cols)
    kv_rows = arrived[:, :, query_cols : query_cols + kv_cols].reshape(own_rows, size * kv_cols)
    head_count = query_rows.shape[1] // HEAD_WIDTH
    kv_heads = kv_rows.shape[1] // (2 * HEAD_WIDTH)
    q_rot = rotate(
        query_rows.reshape(own_rows, head_count, HEAD_WIDTH).astype(jnp.float32), lengths
    ).astype(jnp.bfloat16)
    q_rot = q_rot.reshape(own_rows, kv_heads, head_count // kv_heads, HEAD_WIDTH)
    k_rot = rotate(
        kv_rows[:, : kv_heads * HEAD_WIDTH]
        .reshape(own_rows, kv_heads, HEAD_WIDTH)
        .astype(jnp.float32),
        lengths,
    ).astype(jnp.bfloat16)
    fresh_values = kv_rows[:, kv_heads * HEAD_WIDTH :].reshape(own_rows, kv_heads, HEAD_WIDTH)
    mixed = attend(q_rot, k_rot, fresh_values, rotated_key_cache, earlier_value_cache, lengths)
    head_cols = mixed.shape[1] // size
    leaving = mixed.astype(jnp.float32).reshape(own_rows, size, head_cols).transpose(1, 0, 2)
    heads = exchange(jnp.concatenate([leaving, leaving], 0), size, 3)
    heads = heads.reshape(every_row, head_cols).astype(jnp.bfloat16)
    reduced_output = reduce_and_gather(pick_down(heads, down_weight_output, onehot), size, 4)
    delta_out = pick_up(reduced_output, up_weight_output, onehot).astype(jnp.bfloat16)
    out_cols = delta_out.shape[1]
    own_heads = lax.dynamic_slice_in_dim(heads, replica_at * batch_rows, batch_rows)
    term = jnp.dot(own_heads, output_weight, preferred_element_type=jnp.float32).astype(jnp.bfloat16)
    pieces = term.reshape(size, own_rows, 2, model_width // 2).transpose(0, 2, 1, 3)
    pieces = pieces.reshape(size, 2 * own_rows, model_width // 2)
    deltas = delta_out.reshape(2 * size, own_rows, 2, out_cols // 2).transpose(0, 2, 1, 3)
    deltas = deltas.reshape(2 * size, 2 * own_rows, out_cols // 2)
    total, extra = call(
        functools.partial(output_kernel, size),
        (
            jax.ShapeDtypeStruct(pieces.shape[1:], jnp.float32),
            jax.ShapeDtypeStruct(deltas.shape, jnp.bfloat16),
        ),
        [pltpu.VMEM(pieces.shape, jnp.bfloat16)]
        + [dma((size - 1,))] * 2
        + [dma((2 * size - 1,))] * 2,
        5,
        pieces,
        deltas,
    )
    total = total.reshape(2, own_rows, model_width // 2).transpose(1, 0, 2).reshape(own_rows, model_width)
    extra = extra.reshape(2, size, 2, own_rows, out_cols // 2).astype(jnp.float32)
    extra = (extra[0] + extra[1]).transpose(2, 0, 1, 3).reshape(own_rows, model_width)
    return (total + extra).astype(jnp.bfloat16)


def solution(mesh):
    return jax.shard_map(
        shards,
        mesh=mesh,
        in_specs=(
            P(("parts", "replica", "tensor"), None),
            P(),
            P(("parts", "replica", "tensor")),
            P(("parts", "replica", "tensor")),
            P(("parts", "replica", "tensor"), None, None, None),
            P(("parts", "replica", "tensor"), None, None, None),
            P(None, "tensor"),
            P(None, "tensor"),
            P("tensor", None),
            P("tensor", "replica", None),
            P(None, "replica", "tensor"),
            P(None, "replica", "tensor"),
            P("tensor", "replica", None),
            P(None, "replica", "tensor"),
        ),
        out_specs=P(("parts", "replica", "tensor"), None),
        check_vma=False,
    )
```

time: 310 us -> 135 us (0.44)
  waiting for transfers between devices: 145 us -> 0 us
  Pallas kernels: 0 us -> 95.3 us
  blocking collectives: 87.5 us -> 0 us
  matrix products: 42.5 us -> 23.7 us
  between operations: 14.3 us -> 0.42 us
  starting transfers between devices: 11.2 us -> 0 us
  local copies, waits for them, and re-layouts: 2.58 us -> 9.2 us
    pallas_call x0 -> x6, Pallas kernels: none -> 95.3 us  [call(): pl.pallas_call(kernel, out_shape=outs, in_specs=[pl.BlockSpec(memory_spac...]
    psum x2 -> x0, blocking collectives: 71.3 us -> none  [the longest x1 37.8 us: shards(): lax.psum(pick(features, table_a, onehot), 'tensor').astype(jnp.bfloat16)]
    reduce_scatter x1 -> x0, waiting for transfers between devices: 65.1 us -> none  [shards(): lax.psum_scatter(lax.dynamic_update_slice_in_dim(full_term, column_block...]
    all_gather x5 -> x0, waiting for transfers between devices: 62.9 us -> none  [the longest x1 40.6 us: shards(): lax.all_gather(down_weight_qkv, 'replica', axis=1, tiled=True)]
    dot_general x8, matrix products: 40.8 us -> 22.1 us  [the longest x2 9.55 us: pick_down(): jnp.dot(left_rows, table.reshape(inner_dim, slots * columns), preferred_e...]
    all_to_all x3 -> x0, waiting for transfers between devices: 14.1 us -> none  [the longest x1 6.44 us: shards(): lax.all_to_all(attention_mixed, 'tensor', split_axis=1, concat_axis=0, ti...]
    unnamed x1 -> x0, blocking collectives: 13.9 us -> none
    all_to_all x3 -> x0, starting transfers between devices: 11 us -> none  [the longest x1 4.42 us: shards(): lax.all_to_all(query_part, 'tensor', split_axis=0, concat_axis=1, tiled=T...]
  transfers between devices with their start and end apart: 9 -> 0, of which waited for: 6 -> 0; matrix products, arithmetic and copies ran while one was open for 9% -> 0% of each run, Pallas kernels for 0% -> 0%
where the time goes in v1:
time: 135 us; the launch traced here: 134 us
  Pallas kernels  95.3 us (71%)
  matrix products  23.7 us (18%)
  local copies, waits for them, and re-layouts  9.2 us (7%)
  other arithmetic  5.77 us (4%)
    pallas_call x6, Pallas kernels, call(): pl.pallas_call(kernel, out_shape=outs, in_specs=[pl.BlockSpec(memory_spac...  95.3 us
    dot_general x2, matrix products, pick_down(): jnp.dot(left_rows, table.reshape(inner_dim, slots * columns), preferred_e...  9.55 us
    dot_general x3, matrix products, pick_up(): jnp.dot(spread.reshape(left_rows.shape[0], rank * slots), table.reshape(r...  9.53 us
    reshape x2, local copies, waits for them, and re-layouts, shards(): gathered.reshape(size, size, own_rows, 2, half).transpose(0, 2, 1, 3, 4)  4.86 us

profile of v1, /device:TPU:0, one launch (start us, length us, event | category | flops | bytes accessed | tf_op | source)
XLA Modules:
  0.0 134.4 jit_solution(7180576825760686076)
XLA Ops:
  0.0 1.2 fusion.19
  1.2 1.0 fusion.21
  2.4 0.7 broadcast_in_dim.31.id_ref
  3.2 23.6 %shard_map.136 = (bf16[8,8,16,512]{3,2,1,0:T(8,128)(2,1)S(1)}, bf16[8,16,512]{2,1,0:T(8,128)(2,1)S(1)}, s32[16,8,128]{2,1,0:T(8,128)S(1)}) custom-call(bf16[8,16,512]{2,1,0:T(8,128)(2,1)S(1)} %reshape.354.x_ref, s32[8,128]{1,0:T(8,128)S(1)} %broadcast_in_dim.31.id_ref), custom_call_target="tpu_custom_call" | custom-call | tf_op jit(solution)/shard_map/pallas_call | solution.py:132
  26.8 0.7 reshape_reshape.6
  28.0 8.2 %multiply_reduce_fusion = f32[128,192]{0,1:T(8,128)S(1)} fusion(bf16[1024,32,192]{0,2,1:T(8,128)(2,1)} %param.23, f32[128,32]{0,1:T(8,128)S(1)} %get-tuple-element.26, bf16[64,1024]{1,0:T(8,128)(2,1)S(1)} %reshape_reshape.7, bf16[64,1024]{1,0:T(8,128)(2,1)} %reshape_reshape.6, pred[]{:T(512)S(6)} %eq.34), kind=kOutput, calls=%fused_computation.5 | convolution fusion | flops 1613340672 | bytes 12959745 | tf_op jit(solution)/shard_map/dot_general | solution.py:35
  36.3 13.3 %shard_map.137 = bf16[8,16,256]{2,1,0:T(8,128)(2,1)S(1)} custom-call(f32[8,16,256]{2,1,0:T(8,128)S(1)} %bitcast.123), custom_call_target="tpu_custom_call" | custom-call | tf_op jit(solution)/shard_map/pallas_call | solution.py:132
  49.8 1.4 %convolution_bitcast_fusion = f32[128,128]{0,1:T(8,128)S(1)} fusion(bf16[64,32,128]{2,1,0:T(8,128)(2,1)} %param.24, bf16[128,32]{0,1:T(8,128)(2,1)S(1)} %get-tuple-element.25, bf16[128,64]{0,1:T(8,128)(2,1)S(1)} %copy.43), kind=kOutput, calls=%fused_computation.10 | convolution fusion | flops 67371008 | bytes 614400 | tf_op jit(solution)/shard_map/dot_general | solution.py:45
  51.3 1.2 convolution_bitcast_fusion.1
  52.6 1.4 %reshape.359 = bf16[8,8,8,2,512]{4,3,2,1,0:T(2,128)(2,1)} reshape(bf16[8,8,16,512]{3,2,1,0:T(8,128)(2,1)S(1)} %get-tuple-element.10) | data formatting | bytes 2097152 | tf_op jit(solution)/shard_map/reshape | solution.py:402
  54.0 3.4 %copy.80 = bf16[8,8,8,2,512]{4,3,1,2,0:T(2,128)(2,1)} copy(bf16[8,8,8,2,512]{4,3,2,1,0:T(2,128)(2,1)} %reshape.359) | data formatting | bytes 2097152 | tf_op jit(solution)/shard_map/reshape | solution.py:402
  57.5 1.8 %reshape.360 = bf16[64,8192]{1,0:T(8,128)(2,1)S(1)} reshape(bf16[8,8,8,2,512]{4,3,2,1,0:T(2,128)(2,1)} %bitcast.130) | data formatting | bytes 2097152 | tf_op jit(solution)/shard_map/reshape | solution.py:404
  59.3 2.2 %fusion.71 = f32[64,128]{1,0:T(8,128)S(1)} fusion(bf16[64,8192]{1,0:T(8,128)(2,1)S(1)} %reshape.360, bf16[8192,128]{1,0:T(8,128)(2,1)} %param.20), kind=kOutput, calls=%fused_computation.109 | convolution fusion | flops 134217728 | bytes 3178496 | tf_op jit(solution)/shard_map/dot_general | solution.py:414
  62.1 7.9 %shard_map.138 = f32[16,8,256]{2,1,0:T(8,128)S(1)} custom-call(f32[16,8,256]{2,1,0:T(8,128)S(1)} %bitcast.124), custom_call_target="tpu_custom_call" | custom-call | tf_op jit(solution)/shard_map/pallas_call | solution.py:132
  70.1 0.7 convert_element_type.108
  71.4 0.7 iota_compare_fusion.1
  72.7 1.2 fusion.29
  74.0 7.1 %shard_map.139 = f32[16,8,128]{2,1,0:T(8,128)S(1)} custom-call(f32[16,8,128]{2,1,0:T(8,128)S(1)} %maximum_convert_fusion.x_ref), custom_call_target="tpu_custom_call" | custom-call | tf_op jit(solution)/shard_map/pallas_call | solution.py:132
  81.1 1.4 %fusion.6 = f32[128,64]{0,1:T(8,128)S(1)} fusion(bf16[128,32,64]{0,2,1:T(8,128)(2,1)} %param.26, f32[128,32]{0,1:T(8,128)S(1)} %get-tuple-element.26, f32[16,8,128]{2,1,0:T(8,128)S(1)} %shard_map.139), kind=kOutput, calls=%fused_computation.7 | convolution fusion | flops 67641344 | bytes 638976 | tf_op jit(solution)/shard_map/dot_general | solution.py:35
  82.6 10.1 %shard_map.140 = bf16[8,16,128]{2,1,0:T(8,128)(2,1)S(1)} custom-call(f32[8,16,128]{2,1,0:T(8,128)S(1)} %bitcast.128), custom_call_target="tpu_custom_call" | custom-call | tf_op jit(solution)/shard_map/pallas_call | solution.py:132
  92.8 6.9 %fusion.10 = bf16[128,1024]{1,0:T(8,128)(2,1)S(1)} fusion(bf16[64,32,1024]{2,1,0:T(8,128)(2,1)} %param.27, bf16[128,64]{0,1:T(8,128)(2,1)S(1)} %copy.54, bf16[128,32]{0,1:T(8,128)(2,1)S(1)} %copy-done.4), kind=kOutput, calls=%fused_computation.9 | convolution fusion | flops 537264128 | bytes 4481024 | tf_op jit(solution)/shard_map/dot_general | solution.py:45
  99.7 0.4 convolution_convert_fusion
  100.1 33.4 %shard_map.141 = (f32[16,4096]{1,0:T(8,128)S(1)}, bf16[16,16,512]{2,1,0:T(8,128)(2,1)S(1)}) custom-call(bf16[8,16,4096]{2,1,0:T(8,128)(2,1)S(1)} %bitcast.122, bf16[16,16,512]{2,1,0:T(8,128)(2,1)S(1)} %bitcast.126), custom_call_target="tpu_custom_call" | custom-call | tf_op jit(solution)/shard_map/pallas_call | solution.py:132
  133.7 0.7 add_convert_fusion
  (57 shorter events, 3.4 us)
Async XLA Ops:
  0.0 99.7 %copy-start = (bf16[128,8192]{1,0:T(8,128)(2,1)S(1)}, bf16[128,8192]{1,0:T(8,128)(2,1)}, u32[]{:S(2)}) copy-start(bf16[128,8192]{1,0:T(8,128)(2,1)} %param.22) | copy-start | bytes 6291460
  27.9 23.4 %copy-start.3 = (bf16[128,32]{0,1:T(8,128)(2,1)}, bf16[128,32]{0,1:T(8,128)(2,1)S(1)}, u32[]{:S(2)}) copy-start(bf16[128,32]{0,1:T(8,128)(2,1)S(1)} %get-tuple-element.25) | copy-start | bytes 24580
  59.3 2.2 %copy-start.1 = (bf16[8192,32]{0,1:T(8,128)(2,1)S(1)}, bf16[8192,32]{0,1:T(8,128)(2,1)}, u32[]{:S(2)}) copy-start(bf16[8192,32]{0,1:T(8,128)(2,1)} %param.21) | copy-start | bytes 1572868
  59.3 12.8 %copy-start.2 = (bf16[8,1,128,128]{3,2,1,0:T(8,128)(2,1)S(1)}, bf16[8,1,128,128]{3,2,1,0:T(8,128)(2,1)}, u32[]{:S(2)}) copy-start(bf16[8,1,128,128]{3,2,1,0:T(8,128)(2,1)} %param.18) | copy-start | bytes 786436
  61.9 30.8 %copy-start.4 = (bf16[128,32]{0,1:T(8,128)(2,1)S(1)}, bf16[128,32]{0,1:T(8,128)(2,1)}, u32[]{:S(2)}) copy-start(bf16[128,32]{0,1:T(8,128)(2,1)} %copy-done.3) | copy-start | bytes 24580

commit v2 on v1

--- a/solution.py
+++ b/solution.py
@@ -302,36 +302,165 @@
     swap.wait()
 
 
-def output_kernel(
-    tensor_size, x_ref, d_ref, sum_ref, e_ref, land, send_x, recv_x, send_d, recv_d
+def tail_kernel(
+    size, chunks, rank, ids_ref, x_ref, ao_hbm, wo_hbm, bo_hbm, out_ref,
+    ao, wo, bo, heads_in, red_x, red_land, red_mine, red_all, spread,
+    near, away, land_y, land_z, d_out, d_in,
+    load, send_h, recv_h, send_a, recv_a, send_b, recv_b, send_d, recv_d,
+    send_y, recv_y, send_z, recv_z,
 ):
-    me, everyone = all_peers(tensor_size)
-    tensor, peers = tensor_peers(tensor_size)
+    part, replica, tensor = where_am_i()
+    loads = [
+        pltpu.make_async_copy(src, dst, load.at[at])
+        for at, (src, dst) in enumerate(((ao_hbm, ao), (wo_hbm, wo), (bo_hbm, bo)))
+    ]
+    for copy in loads:
+        copy.start()
+    me, everyone = all_peers(size)
+    _, peers = tensor_peers(size)
     greet([peer for _, peer in everyone])
-    copies = []
+    depth = size // 2
+    level, side = tensor // 2, lax.rem(tensor, 2)
+    across = (part, replica, level * 2 + 1 - side)
+    rows = heads_in.shape[1]
+    batch = rows * size
+    every = 2 * batch
+    model = out_ref.shape[1]
+    half = model // 2
+    slots = bo.shape[0] // rank
+
+    sent = []
+    for step, (other, peer) in enumerate(everyone):
+        copy = remote(
+            x_ref.at[lax.rem(other, size)], heads_in.at[me], send_h.at[step], recv_h.at[step], peer
+        )
+        copy.start()
+        sent.append(copy)
+    heads_in[me] = x_ref[tensor]
+    for copy in sent:
+        copy.wait()
+    heads = heads_in[...].reshape(every, heads_in.shape[2]).astype(jnp.bfloat16)
+    local_id = ids_ref[:, :1] - replica * slots
+    loads[0].wait()
+    wide = 512
+    total = None
+    for at in range(0, ao.shape[0], wide):
+        product = lax.dot_general(
+            heads, ao[at : at + wide, :], (((1,), (1,)), ((), ())), preferred_element_type=jnp.float32
+        )
+        first = lax.broadcasted_iota(jnp.int32, product.shape, 1) + at - local_id * rank
+        product = jnp.where(jnp.logical_and(first >= 0, first < rank), product, 0.0)
+        for lane in range(0, wide, 128):
+            piece = product[:, lane : lane + 128]
+            total = piece if total is None else total + piece
+    if rank == 64:
+        total = total + pltpu.roll(total, 64, 1)
+    red_x[...] = total.reshape(red_x.shape)
+    sent = []
     for step, (other, peer) in enumerate(peers):
-        copy = remote(x_ref.at[other], land.at[tensor], send_x.at[step], recv_x.at[step], peer)
-        copy.start()
-        copies.append(copy)
+        copy = remote(red_x.at[other], red_land.at[tensor], send_a.at[step], recv_a.at[step], peer)
+        copy.start()
+        sent.append(copy)
+    red_land[tensor] = red_x[tensor]
+
+    own = heads_in[pl.ds(replica * size, size)].reshape(batch, heads_in.shape[2]).astype(jnp.bfloat16)
+    loads[1].wait()
+    width = half // chunks
+    y_copies = []
+    for chunk in range(chunks):
+        parts = []
+        for start in (chunk * width, half + chunk * width):
+            term = jnp.dot(own, wo[:, start : start + width], preferred_element_type=jnp.float32)
+            parts.append(term.reshape(size, rows, width))
+        term = jnp.concatenate(parts, 1).reshape(depth, 2, 2 * rows, width)
+        here = jnp.where(side == 0, term[:, 0], term[:, 1])
+        there = jnp.where(side == 0, term[:, 1], term[:, 0])
+        away[chunk] = there.astype(jnp.bfloat16)
+        copy = remote(away.at[chunk], land_y.at[chunk], send_y.at[chunk], recv_y.at[chunk], across)
+        copy.start()
+        y_copies.append(copy)
+        near[chunk] = here
+
+    for copy in sent:
+        copy.wait()
+    total = red_land[0]
+    for step in range(1, size):
+        total = total + red_land[step]
+    red_mine[...] = total.astype(jnp.bfloat16)
+    sent = []
+    for step, (other, peer) in enumerate(peers):
+        copy = remote(red_mine, red_all.at[tensor], send_b.at[step], recv_b.at[step], peer)
+        copy.start()
+        sent.append(copy)
+    red_all[tensor] = red_mine[...]
+
+    z_copies = []
+
+    def pass_on(chunk):
+        y_copies[chunk].wait()
+        near[chunk] = near[chunk] + land_y[chunk].astype(jnp.float32)
+        away[chunk] = near[chunk].astype(jnp.bfloat16)
+        for step in range(1, depth):
+            other = lax.rem(level + step, depth)
+            copy = remote(
+                away.at[chunk, other], land_z.at[chunk, level],
+                send_z.at[chunk, step - 1], recv_z.at[chunk, step - 1],
+                (part, replica, other * 2 + side),
+            )
+            copy.start()
+            z_copies.append(copy)
+        land_z[chunk, level] = away[chunk, level]
+
+    early = min(1, chunks)
+    for chunk in range(early):
+        pass_on(chunk)
+    for copy in sent:
+        copy.wait()
+    shrunk = red_all[...].reshape(every, red_all.shape[2])
+    for at in range(0, bo.shape[0], wide):
+        shape = (shrunk.shape[1], wide)
+        place = lax.broadcasted_iota(jnp.int32, shape, 1) + at
+        place = place - lax.broadcasted_iota(jnp.int32, shape, 0) * slots
+        expand = jnp.where(jnp.logical_and(place >= 0, place < slots), 1.0, 0.0).astype(jnp.bfloat16)
+        piece = jnp.dot(shrunk, expand, preferred_element_type=jnp.float32)
+        slot = lax.rem(lax.broadcasted_iota(jnp.int32, piece.shape, 1), slots)
+        spread[:, at : at + wide] = jnp.where(slot == local_id, piece, 0.0).astype(jnp.bfloat16)
+    loads[2].wait()
+    cols = bo.shape[1]
+    delta = jnp.concatenate(
+        [
+            jnp.dot(
+                spread[...], bo[:, at : at + cols // 2], preferred_element_type=jnp.float32
+            ).reshape(2 * size, rows, cols // 2)
+            for at in (0, cols // 2)
+        ],
+        1,
+    )
+    d_out[...] = delta.astype(jnp.bfloat16)
+    d_copies = []
     for step, (other, peer) in enumerate(everyone):
-        copy = remote(d_ref.at[other], e_ref.at[me], send_d.at[step], recv_d.at[step], peer)
-        copy.start()
-        copies.append(copy)
-    land[tensor] = x_ref[tensor]
-    e_ref[me] = d_ref[me]
-    for copy in copies:
-        copy.wait()
-    width = 512
-
-    def column(at, carry):
-        spot = pl.ds(pl.multiple_of(at * width, width), width)
-        total = land[0, :, spot].astype(jnp.float32)
-        for step in range(1, tensor_size):
-            total = total + land[step, :, spot].astype(jnp.float32)
-        sum_ref[:, spot] = total
-        return carry
-
-    lax.fori_loop(0, sum_ref.shape[1] // width, column, 0)
+        copy = remote(d_out.at[other], d_in.at[me], send_d.at[step], recv_d.at[step], peer)
+        copy.start()
+        d_copies.append(copy)
+    d_in[me] = d_out[me]
+    for chunk in range(early, chunks):
+        pass_on(chunk)
+    count = depth - 1
+    for chunk in range(chunks):
+        for copy in z_copies[chunk * count : (chunk + 1) * count]:
+            copy.wait()
+        total = land_z[chunk, 0].astype(jnp.float32)
+        for at in range(1, depth):
+            total = total + land_z[chunk, at].astype(jnp.float32)
+        out_ref[:, chunk * width : (chunk + 1) * width] = total[:rows]
+        out_ref[:, half + chunk * width : half + (chunk + 1) * width] = total[rows:]
+    for copy in d_copies:
+        copy.wait()
+    for at in range(size):
+        extra = d_in[at].astype(jnp.float32) + d_in[size + at].astype(jnp.float32)
+        start = at * cols
+        out_ref[:, start : start + cols // 2] += extra[:rows]
+        out_ref[:, start + cols // 2 : start + cols] += extra[rows:]
 
 
 def fold_slices(rows, slices):
@@ -456,34 +585,53 @@
     mixed = attend(q_rot, k_rot, fresh_values, rotated_key_cache, earlier_value_cache, lengths)
     head_cols = mixed.shape[1] // size
     leaving = mixed.astype(jnp.float32).reshape(own_rows, size, head_cols).transpose(1, 0, 2)
-    heads = exchange(jnp.concatenate([leaving, leaving], 0), size, 3)
-    heads = heads.reshape(every_row, head_cols).astype(jnp.bfloat16)
-    reduced_output = reduce_and_gather(pick_down(heads, down_weight_output, onehot), size, 4)
-    delta_out = pick_up(reduced_output, up_weight_output, onehot).astype(jnp.bfloat16)
-    out_cols = delta_out.shape[1]
-    own_heads = lax.dynamic_slice_in_dim(heads, replica_at * batch_rows, batch_rows)
-    term = jnp.dot(own_heads, output_weight, preferred_element_type=jnp.float32).astype(jnp.bfloat16)
-    pieces = term.reshape(size, own_rows, 2, model_width // 2).transpose(0, 2, 1, 3)
-    pieces = pieces.reshape(size, 2 * own_rows, model_width // 2)
-    deltas = delta_out.reshape(2 * size, own_rows, 2, out_cols // 2).transpose(0, 2, 1, 3)
-    deltas = deltas.reshape(2 * size, 2 * own_rows, out_cols // 2)
-    total, extra = call(
-        functools.partial(output_kernel, size),
-        (
-            jax.ShapeDtypeStruct(pieces.shape[1:], jnp.float32),
-            jax.ShapeDtypeStruct(deltas.shape, jnp.bfloat16),
+    rank_out, _, out_cols = up_weight_output.shape
+    down_table = down_weight_output.transpose(1, 2, 0).reshape(-1, head_cols)
+    up_table = up_weight_output.reshape(rank_out * slots, out_cols)
+    chunks = 4
+    width = model_width // 2 // chunks
+    double = 2 * own_rows
+    vmem, f32, bf16 = pltpu.VMEM, jnp.float32, jnp.bfloat16
+    out = pl.pallas_call(
+        functools.partial(tail_kernel, size, chunks, rank_out),
+        out_shape=jax.ShapeDtypeStruct((own_rows, model_width), f32),
+        in_specs=[pl.BlockSpec(memory_space=vmem)] * 2 + [pl.BlockSpec(memory_space=pl.ANY)] * 3,
+        out_specs=pl.BlockSpec(memory_space=vmem),
+        scratch_shapes=[
+            vmem(down_table.shape, bf16),
+            vmem(output_weight.shape, bf16),
+            vmem(up_table.shape, bf16),
+            vmem((2 * size, own_rows, head_cols), f32),
+            vmem((size, double, 128), f32),
+            vmem((size, double, 128), f32),
+            vmem((double, 128), bf16),
+            vmem((size, double, 128), bf16),
+            vmem((every_row, rank_out * slots), bf16),
+            vmem((chunks, depth, double, width), f32),
+            vmem((chunks, depth, double, width), bf16),
+            vmem((chunks, depth, double, width), bf16),
+            vmem((chunks, depth, double, width), bf16),
+            vmem((2 * size, double, out_cols // 2), bf16),
+            vmem((2 * size, double, out_cols // 2), bf16),
+            dma((3,)),
+            dma((2 * size - 1,)),
+            dma((2 * size - 1,)),
+            dma((size - 1,)),
+            dma((size - 1,)),
+            dma((size - 1,)),
+            dma((size - 1,)),
+            dma((2 * size - 1,)),
+            dma((2 * size - 1,)),
+            dma((chunks,)),
+            dma((chunks,)),
+            dma((chunks, steps)),
+            dma((chunks, steps)),
+        ],
+        compiler_params=pltpu.CompilerParams(
+            collective_id=3, has_side_effects=True, vmem_limit_bytes=VMEM_LIMIT
         ),
-        [pltpu.VMEM(pieces.shape, jnp.bfloat16)]
-        + [dma((size - 1,))] * 2
-        + [dma((2 * size - 1,))] * 2,
-        5,
-        pieces,
-        deltas,
-    )
-    total = total.reshape(2, own_rows, model_width // 2).transpose(1, 0, 2).reshape(own_rows, model_width)
-    extra = extra.reshape(2, size, 2, own_rows, out_cols // 2).astype(jnp.float32)
-    extra = (extra[0] + extra[1]).transpose(2, 0, 1, 3).reshape(own_rows, model_width)
-    return (total + extra).astype(jnp.bfloat16)
+    )(id_tiles.reshape(every_row, 128), leaving, down_table, output_weight, up_table)
+    return out.astype(jnp.bfloat16)
 
 
 def solution(mesh):

time: 135 us -> 113 us (0.84)
  Pallas kernels: 95.3 us -> 82.8 us
  matrix products: 23.7 us -> 15.4 us
  other arithmetic: 5.77 us -> 4.32 us
    pallas_call x6 -> x3, Pallas kernels: 95.3 us -> 44.7 us  [call(): pl.pallas_call(kernel, out_shape=outs, in_specs=[pl.BlockSpec(memory_spac...]
    pallas_call x0 -> x1, Pallas kernels: none -> 38.1 us  [shards(): pl.pallas_call(functools.partial(tail_kernel, size, chunks, rank_out), ou...]
    dot_general x3 -> x2, matrix products: 9.53 us -> 2.63 us  [pick_up(): jnp.dot(spread.reshape(left_rows.shape[0], rank * slots), table.reshape(r...]
    unnamed x12 -> x15, local copies, waits for them, and re-layouts: 0.21 us -> 2.6 us
    dot_general x2 -> x1, matrix products: 9.55 us -> 8.82 us  [pick_down(): jnp.dot(left_rows, table.reshape(inner_dim, slots * columns), preferred_e...]
where the time goes in v2:
time: 113 us
  Pallas kernels  82.8 us (73%)
  matrix products  15.4 us (14%)
  local copies, waits for them, and re-layouts  10.1 us (9%)
  other arithmetic  4.32 us (4%)
    pallas_call x3, Pallas kernels, call(): pl.pallas_call(kernel, out_shape=outs, in_specs=[pl.BlockSpec(memory_spac...  44.7 us
    pallas_call x1, Pallas kernels, shards(): pl.pallas_call(functools.partial(tail_kernel, size, chunks, rank_out), ou...  38.1 us
    dot_general x1, matrix products, pick_down(): jnp.dot(left_rows, table.reshape(inner_dim, slots * columns), preferred_e...  8.82 us
    reshape x2, local copies, waits for them, and re-layouts, shards(): gathered.reshape(size, size, own_rows, 2, half).transpose(0, 2, 1, 3, 4)  3.61 us
    dot_general x2, matrix products, pick_up(): jnp.dot(spread.reshape(left_rows.shape[0], rank * slots), table.reshape(r...  2.63 us
    unnamed x15, local copies, waits for them, and re-layouts  2.6 us

profile of v2, /device:TPU:0, one launch (start us, length us, event | category | flops | bytes accessed | tf_op | source)
XLA Modules:
  0.0 112.9 jit_solution(17064840061955189447)
XLA Ops:
  0.0 1.2 %fusion.8 = f32[8]{0:T(128)S(1)} fusion(bf16[8,8192]{1,0:T(8,128)(2,1)} %param.14), kind=kLoop, calls=%fused_computation.13 | loop fusion | flops 196600 | bytes 131104 | tf_op jit(solution)/shard_map/reduce_sum | solution.py:495
  1.2 1.0 fusion.10
  2.4 0.7 broadcast_in_dim.30.id_ref
  3.2 23.6 %shard_map.136 = (bf16[8,8,16,512]{3,2,1,0:T(8,128)(2,1)S(1)}, bf16[8,16,512]{2,1,0:T(8,128)(2,1)S(1)}, s32[16,8,128]{2,1,0:T(8,128)S(1)}) custom-call(bf16[8,16,512]{2,1,0:T(8,128)(2,1)S(1)} %reshape.318.x_ref, s32[8,128]{1,0:T(8,128)S(1)} %broadcast_in_dim.30.id_ref), custom_call_target="tpu_custom_call" | custom-call | tf_op jit(solution)/shard_map/pallas_call | solution.py:132
  26.8 0.7 reshape_reshape.6
  27.5 0.3 subtract_reduce_fusion
  28.0 8.8 %multiply_reduce_fusion = f32[128,192]{0,1:T(8,128)} fusion(bf16[1024,32,192]{0,2,1:T(8,128)(2,1)} %param.23, f32[128,32]{0,1:T(8,128)S(1)} %get-tuple-element.22, bf16[64,1024]{1,0:T(8,128)(2,1)S(1)} %reshape_reshape.7, bf16[64,1024]{1,0:T(8,128)(2,1)} %reshape_reshape.6, pred[]{:T(512)S(6)} %eq.34), kind=kOutput, calls=%fused_computation.2 | convolution fusion | flops 1613340672 | bytes 12959745 | tf_op jit(solution)/shard_map/dot_general | solution.py:35
  36.8 1.0 copy.52
  37.8 13.3 %shard_map.137 = bf16[8,16,256]{2,1,0:T(8,128)(2,1)S(1)} custom-call(f32[8,16,256]{2,1,0:T(8,128)S(1)} %bitcast.90), custom_call_target="tpu_custom_call" | custom-call | tf_op jit(solution)/shard_map/pallas_call | solution.py:132
  51.3 1.4 %convolution_bitcast_fusion = f32[128,128]{0,1:T(8,128)S(1)} fusion(bf16[64,32,128]{2,1,0:T(8,128)(2,1)} %param.24, bf16[128,32]{0,1:T(8,128)(2,1)S(1)} %get-tuple-element.21, bf16[128,64]{0,1:T(8,128)(2,1)S(1)} %copy.39), kind=kOutput, calls=%fused_computation.3 | convolution fusion | flops 67371008 | bytes 614400 | tf_op jit(solution)/shard_map/dot_general | solution.py:45
  52.8 1.2 %convolution_bitcast_fusion.1 = f32[128,32]{0,1:T(8,128)S(1)} fusion(bf16[64,32,32]{0,2,1:T(8,128)(2,1)} %param.25, bf16[128,64]{0,1:T(8,128)(2,1)S(1)} %copy.41, bf16[128,32]{0,1:T(8,128)(2,1)S(1)} %get-tuple-element.21), kind=kOutput, calls=%fused_computation.6 | convolution fusion | flops 17039360 | bytes 172032 | tf_op jit(solution)/shard_map/dot_general | solution.py:45
  54.1 1.2 %reshape.324 = bf16[8,8,8,2,512]{4,3,2,1,0:T(2,128)(2,1)} reshape(bf16[8,8,16,512]{3,2,1,0:T(8,128)(2,1)S(1)} %get-tuple-element.9) | data formatting | bytes 2097152 | tf_op jit(solution)/shard_map/reshape | solution.py:531
  55.4 2.4 %copy.68 = bf16[8,8,8,2,512]{4,3,1,2,0:T(2,128)(2,1)S(1)} copy(bf16[8,8,8,2,512]{4,3,2,1,0:T(2,128)(2,1)} %reshape.324) | data formatting | bytes 2097152 | tf_op jit(solution)/shard_map/reshape | solution.py:531
  57.7 1.6 %reshape.325 = bf16[64,8192]{1,0:T(8,128)(2,1)} reshape(bf16[8,8,8,2,512]{4,3,2,1,0:T(2,128)(2,1)S(1)} %bitcast.94) | data formatting | bytes 2097152 | tf_op jit(solution)/shard_map/reshape | solution.py:533
  59.4 1.9 %fusion.55 = f32[64,128]{1,0:T(8,128)S(1)} fusion(bf16[64,8192]{1,0:T(8,128)(2,1)} %reshape.325, bf16[8192,128]{1,0:T(8,128)(2,1)S(1)} %copy-done), kind=kOutput, calls=%fused_computation.91 | convolution fusion | flops 134217728 | bytes 3178496 | tf_op jit(solution)/shard_map/dot_general | solution.py:543
  61.3 0.4 fusion.56
  61.9 7.9 %shard_map.138 = f32[16,8,256]{2,1,0:T(8,128)S(1)} custom-call(f32[16,8,256]{2,1,0:T(8,128)S(1)} %bitcast.89), custom_call_target="tpu_custom_call" | custom-call | tf_op jit(solution)/shard_map/pallas_call | solution.py:132
  70.4 0.1 fusion.33
  70.6 0.3 fusion.54
  70.9 0.2 fusion.28
  71.2 1.2 %fusion.18 = f32[8,8,128]{2,1,0:T(8,128)S(1)} fusion(bf16[8,1,128,128]{3,2,1,0:T(8,128)(2,1)} %param.19, f32[8,8,128]{2,1,0:T(8,128)S(1)} %get-tuple-element.24, f32[8,8]{1,0:T(8,128)S(1)} %exponential_add_fusion, f32[8,8]{1,0:T(8,128)S(1)} %multiply_maximum_fusion), kind=kOutput, calls=%fused_computation.23 | convolution fusion | flops 2121728 | bytes 328192 | tf_op jit(solution)/shard_map/rgjl,rgld->rgjd/dot_general | solution.py:70
  72.5 1.6 %copy-done.1 = bf16[128,8192]{1,0:T(8,128)(2,1)S(1)} copy-done((bf16[128,8192]{1,0:T(8,128)(2,1)S(1)}, bf16[128,8192]{1,0:T(8,128)(2,1)}, u32[]{:S(2)}) %copy-start.1) | copy-done | bytes 2097176
  74.1 38.1 %shard_map.139 = f32[8,8192]{1,0:T(8,128)S(1)} custom-call(s32[128,128]{1,0:T(8,128)S(1)} %bitcast.92, f32[8,8,128]{2,1,0:T(8,128)S(1)} %fusion.29.x_ref, bf16[2048,128]{1,0:T(8,128)(2,1)S(1)} %bitcast.88, bf16[128,8192]{1,0:T(8,128)(2,1)S(1)} %copy-done.1, bf16[2048,1024]{1,0:T(8,128)(2,1)} %bitcast.93), custom_call_target="tpu_custom_call" | custom-call | tf_op jit(solution)/shard_map/pallas_call | solution.py:595
  112.2 0.7 convert_element_type.99
  (49 shorter events, 1.7 us)
Async XLA Ops:
  0.0 59.4 %copy-start = (bf16[8192,128]{1,0:T(8,128)(2,1)S(1)}, bf16[8192,128]{1,0:T(8,128)(2,1)}, u32[]{:S(2)}) copy-start(bf16[8192,128]{1,0:T(8,128)(2,1)} %param.20) | copy-start | bytes 6291460
  59.4 1.9 %copy-start.3 = (bf16[64,8192]{1,0:T(8,128)(2,1)S(1)}, bf16[64,8192]{1,0:T(8,128)(2,1)}, u32[]{:S(2)}) copy-start(bf16[64,8192]{1,0:T(8,128)(2,1)} %reshape.325) | copy-start | bytes 3145732
  59.4 1.9 %copy-start.4 = (bf16[8192,32]{0,1:T(8,128)(2,1)S(1)}, bf16[8192,32]{0,1:T(8,128)(2,1)}, u32[]{:S(2)}) copy-start(bf16[8192,32]{0,1:T(8,128)(2,1)} %param.21) | copy-start | bytes 1572868
  59.4 10.5 %copy-start.6 = (s32[8]{0:T(128)S(1)}, s32[8]{0:T(128)}, u32[]{:S(2)}) copy-start(s32[8]{0:T(128)} %param.17) | copy-start | bytes 100
  59.4 11.2 %copy-start.5 = (bf16[8,1,128,128]{3,2,1,0:T(8,128)(2,1)S(1)}, bf16[8,1,128,128]{3,2,1,0:T(8,128)(2,1)}, u32[]{:S(2)}) copy-start(bf16[8,1,128,128]{3,2,1,0:T(8,128)(2,1)} %param.18) | copy-start | bytes 786436
  59.4 13.1 %copy-start.2 = (bf16[128,32,64]{0,2,1:T(8,128)(2,1)S(1)}, bf16[128,32,64]{0,2,1:T(8,128)(2,1)}, u32[]{:S(2)}) copy-start(bf16[128,32,64]{0,2,1:T(8,128)(2,1)} %param.26) | copy-start | bytes 1572868
  72.5 1.6 %copy-start.1 = (bf16[128,8192]{1,0:T(8,128)(2,1)S(1)}, bf16[128,8192]{1,0:T(8,128)(2,1)}, u32[]{:S(2)}) copy-start(bf16[128,8192]{1,0:T(8,128)(2,1)} %wo_hbm.1) | copy-start | bytes 6291460

commit v3 on v2

--- a/solution.py
+++ b/solution.py
@@ -30,25 +30,6 @@
     )
 
 
-def pick_down(left_rows, table, onehot):
-    inner_dim, slots, columns = table.shape
-    product = jnp.dot(
-        left_rows, table.reshape(inner_dim, slots * columns), preferred_element_type=jnp.float32
-    )
-    product = product.reshape(left_rows.shape[0], slots, columns)
-    return jnp.sum(product * onehot[:, :, None], axis=1)
-
-
-def pick_up(left_rows, table, onehot):
-    rank, slots, columns = table.shape
-    spread = left_rows[:, :, None] * onehot.astype(left_rows.dtype)[:, None, :]
-    return jnp.dot(
-        spread.reshape(left_rows.shape[0], rank * slots),
-        table.reshape(rank * slots, columns),
-        preferred_element_type=jnp.float32,
-    )
-
-
 def attend(q_rot, k_rot, fresh_values, rotated_key_cache, earlier_value_cache, lengths):
     score_scale = HEAD_WIDTH ** (-0.5)
     scores = (
@@ -115,99 +96,60 @@
     )
 
 
-def exchange_kernel(tensor_size, x_ref, y_ref, send_sem, recv_sem):
-    me, peers = all_peers(tensor_size)
-    greet([peer for _, peer in peers])
-    copies = []
-    for step, (other, peer) in enumerate(peers):
-        copy = remote(x_ref.at[other], y_ref.at[me], send_sem.at[step], recv_sem.at[step], peer)
-        copy.start()
-        copies.append(copy)
-    y_ref[me] = x_ref[me]
-    for copy in copies:
-        copy.wait()
-
-
-def call(kernel, outs, scratch, collective_id, *operands):
-    return pl.pallas_call(
-        kernel,
-        out_shape=outs,
-        in_specs=[pl.BlockSpec(memory_space=pltpu.VMEM)] * len(operands),
-        out_specs=jax.tree.map(lambda _: pl.BlockSpec(memory_space=pltpu.VMEM), outs),
-        scratch_shapes=scratch,
-        compiler_params=pltpu.CompilerParams(
-            collective_id=collective_id, has_side_effects=True, vmem_limit_bytes=VMEM_LIMIT
-        ),
-    )(*operands)
-
-
-def exchange(x, tensor_size, collective_id):
-    count = 2 * tensor_size - 1
-    return call(
-        functools.partial(exchange_kernel, tensor_size),
-        jax.ShapeDtypeStruct(x.shape, x.dtype),
-        [pltpu.SemaphoreType.DMA((count,)), pltpu.SemaphoreType.DMA((count,))],
-        collective_id,
-        x,
-    )
-
-
-def reduce_kernel(tensor_size, x_ref, y_ref, land, mine, send_a, recv_a, send_b, recv_b):
-    me, peers = tensor_peers(tensor_size)
-    greet([peer for _, peer in peers])
-    copies = []
-    for step, (other, peer) in enumerate(peers):
-        copy = remote(x_ref.at[other], land.at[me], send_a.at[step], recv_a.at[step], peer)
-        copy.start()
-        copies.append(copy)
-    land[me] = x_ref[me]
-    for copy in copies:
-        copy.wait()
-    total = land[0]
-    for step in range(1, tensor_size):
-        total = total + land[step]
-    mine[...] = total.astype(mine.dtype)
-    copies = []
-    for step, (other, peer) in enumerate(peers):
-        copy = remote(mine, y_ref.at[me], send_b.at[step], recv_b.at[step], peer)
-        copy.start()
-        copies.append(copy)
-    y_ref[me] = mine[...]
-    for copy in copies:
-        copy.wait()
-
-
-def reduce_and_gather(x, tensor_size, collective_id):
-    rows, width = x.shape
-    padded = -(-width // 128) * 128
-    blocks = jnp.pad(x, ((0, 0), (0, padded - width))).reshape(
-        tensor_size, rows // tensor_size, padded
-    )
-    count = tensor_size - 1
-    done = call(
-        functools.partial(reduce_kernel, tensor_size),
-        jax.ShapeDtypeStruct(blocks.shape, jnp.bfloat16),
-        [pltpu.VMEM(blocks.shape, jnp.float32), pltpu.VMEM(blocks.shape[1:], jnp.bfloat16)]
-        + [pltpu.SemaphoreType.DMA((count,))] * 4,
-        collective_id,
-        blocks,
-    )
-    return done.reshape(rows, padded)[:, :width]
-
-
-def gather_kernel(
-    tensor_size, x_ref, id_ref, g_ref, fo_ref, ids_ref,
-    send_id, recv_id, send_up, recv_up, send_dn, recv_dn, send_y, recv_y, send_f, recv_f,
+def head_kernel(
+    size, rank, x_ref, id_ref, a_hbm, wq_hbm, wkv_hbm, bq_hbm, bkv_hbm, out_ref, ids_ref,
+    a_all, wq, wkv, bq, bkv, folded, g_ref, feat_in, features, shrink,
+    red_x, red_land, red_mine, red_all, spread, out_x, out_in,
+    load_a, load, send_id, recv_id, send_ft, recv_ft, send_up, recv_up, send_dn, recv_dn,
+    send_y, recv_y, send_a, recv_a, send_b, recv_b, send_o, recv_o,
 ):
     part, replica, tensor = where_am_i()
-    me, peers = all_peers(tensor_size)
-    greet([peer for _, peer in peers])
-    depth = tensor_size // 2
+    loads = [
+        pltpu.make_async_copy(src, dst, load.at[at])
+        for at, (src, dst) in enumerate(
+            ((wq_hbm, wq), (wkv_hbm, wkv), (bq_hbm, bq), (bkv_hbm, bkv))
+        )
+    ]
+    pair = 6 * rank
+    pairs = a_all.shape[0] // pair
+
+    def load_pair(at):
+        spot = pl.ds(pl.multiple_of(at * pair, pair), pair)
+        return pltpu.make_async_copy(a_hbm.at[spot], a_all.at[spot], load_a.at[at])
+
+    for at in range(pairs):
+        load_pair(at).start()
+    for copy in loads:
+        copy.start()
+    rows, model = x_ref.shape
+    batch = rows * size
+    every = 2 * batch
+    part_cols = model // size
+    half = part_cols // 2
+    for at in range(size):
+        lo = x_ref[:, at * part_cols : at * part_cols + half]
+        hi = x_ref[:, at * part_cols + half : (at + 1) * part_cols]
+        folded[at] = jnp.concatenate([lo, hi], 0).astype(jnp.bfloat16)
+    me, everyone = all_peers(size)
+    _, peers = tensor_peers(size)
+    greet([peer for _, peer in everyone])
+    copies = []
+    for step, (other, peer) in enumerate(everyone):
+        copy = remote(
+            folded.at[lax.rem(other, size)], feat_in.at[me], send_ft.at[step], recv_ft.at[step], peer
+        )
+        copy.start()
+        copies.append(copy)
+        copy = remote(id_ref, ids_ref.at[me], send_id.at[step], recv_id.at[step], peer)
+        copy.start()
+        copies.append(copy)
+    feat_in[me] = folded[tensor]
+    ids_ref[me] = id_ref[...]
+    depth = size // 2
     level, side = tensor // 2, lax.rem(tensor, 2)
-    above = (part, replica, lax.rem(tensor + 2, tensor_size))
-    below = (part, replica, lax.rem(tensor + tensor_size - 2, tensor_size))
+    above = (part, replica, lax.rem(tensor + 2, size))
+    below = (part, replica, lax.rem(tensor + size - 2, size))
     across = (part, replica, level * 2 + 1 - side)
-    twin = (part, 1 - replica, tensor)
 
     def block(at):
         return jnp.clip(at, 0, depth - 1) * 2 + side
@@ -239,7 +181,7 @@
             g_ref.at[at * 2 + 1 - side], g_ref.at[at * 2 + 1 - side], send_y.at[at], recv_y.at[at], across
         )
 
-    g_ref[tensor] = x_ref[...]
+    g_ref[tensor] = folded[...]
     has_above, has_below = level < depth - 1, level > 0
 
     @pl.when(has_above)
@@ -251,12 +193,22 @@
         down(0).start()
 
     cross(level).start()
-    copies = []
-    for step, (other, peer) in enumerate(peers):
-        copy = remote(id_ref, ids_ref.at[me], send_id.at[step], recv_id.at[step], peer)
-        copy.start()
-        copies.append(copy)
-    ids_ref[me] = id_ref[...]
+    slots = bq.shape[0] // rank
+
+    def shrink_step(at, carry):
+        load_pair(at).wait()
+        spot = pl.ds(pl.multiple_of(at * pair, pair), pair)
+        product = lax.dot_general(
+            features[...], a_all[spot, :], (((1,), (1,)), ((), ())),
+            preferred_element_type=jnp.float32,
+        )
+        local = ids_ref[...].reshape(every, 128)[:, :1] - replica * slots
+        first = lax.broadcasted_iota(jnp.int32, product.shape, 1) + (2 * at - local) * (3 * rank)
+        shrink[...] += jnp.where(
+            jnp.logical_and(first >= 0, first < 3 * rank), product, 0.0
+        )
+        return carry
+
     for step in range(depth - 1):
 
         @pl.when(level - step - 1 >= 0)
@@ -281,10 +233,110 @@
 
             cross(level + step + 1).start()
 
+        if step == 0:
+            for copy in copies:
+                copy.wait()
+            taken = feat_in[...].astype(jnp.float32)
+            features[:, :half] = taken[:, :rows].reshape(every, half).astype(jnp.bfloat16)
+            features[:, half:] = taken[:, rows:].reshape(every, half).astype(jnp.bfloat16)
+            shrink[...] = jnp.zeros_like(shrink)
+        lax.fori_loop(
+            step * pairs // (depth - 1), (step + 1) * pairs // (depth - 1), shrink_step, 0
+        )
+
+    total = shrink[...]
+    third = 3 * rank
+    total = total[:, :third] + total[:, third:]
+    total = jnp.concatenate([total, jnp.zeros((every, red_x.shape[2] - third), jnp.float32)], 1)
+    red_x[...] = total.reshape(red_x.shape)
+    sent = []
+    for step, (other, peer) in enumerate(peers):
+        copy = remote(red_x.at[other], red_land.at[tensor], send_a.at[step], recv_a.at[step], peer)
+        copy.start()
+        sent.append(copy)
+    red_land[tensor] = red_x[tensor]
+    for copy in sent:
+        copy.wait()
+    total = red_land[0]
+    for step in range(1, size):
+        total = total + red_land[step]
+    red_mine[...] = total.astype(jnp.bfloat16)
+    sent = []
+    for step, (other, peer) in enumerate(peers):
+        copy = remote(red_mine, red_all.at[tensor], send_b.at[step], recv_b.at[step], peer)
+        copy.start()
+        sent.append(copy)
+    red_all[tensor] = red_mine[...]
+
     for at in range(depth):
         cross_in(at).wait_recv()
-    swap = remote(g_ref.at[:, tensor], fo_ref, send_f, recv_f, twin)
-    swap.start()
+    loads[0].wait()
+    loads[1].wait()
+    qcols, kvcols = wq.shape[1], wkv.shape[0]
+
+    def base_step(at, carry):
+        base_q, base_kv = carry
+        taken = g_ref[:, at].astype(jnp.float32)
+        for side_at in range(2):
+            left = taken[:, side_at * rows : (side_at + 1) * rows].reshape(batch, half)
+            left = left.astype(jnp.bfloat16)
+            spot = pl.ds(pl.multiple_of(at * part_cols + side_at * half, half), half)
+            base_q = base_q + jnp.dot(left, wq[spot, :], preferred_element_type=jnp.float32)
+            base_kv = base_kv + lax.dot_general(
+                left, wkv[:, spot], (((1,), (1,)), ((), ())), preferred_element_type=jnp.float32
+            )
+        return base_q, base_kv
+
+    base_q, base_kv = lax.fori_loop(
+        0, size, base_step,
+        (jnp.zeros((batch, qcols), jnp.float32), jnp.zeros((batch, kvcols), jnp.float32)),
+    )
+    for copy in sent:
+        copy.wait()
+    shrunk = red_all[...].reshape(every, red_all.shape[2])
+    local_id = ids_ref[...].reshape(every, 128)[:, :1] - replica * slots
+    wide = 512
+    for at in range(0, bq.shape[0], wide):
+        place = lax.broadcasted_iota(jnp.int32, (rank, wide), 1) + at
+        place = place - lax.broadcasted_iota(jnp.int32, (rank, wide), 0) * slots
+        expand = jnp.where(jnp.logical_and(place >= 0, place < slots), 1.0, 0.0).astype(jnp.bfloat16)
+        piece = jnp.dot(shrunk[:, :rank], expand, preferred_element_type=jnp.float32)
+        slot = lax.rem(lax.broadcasted_iota(jnp.int32, piece.shape, 1), slots)
+        spread[:, at : at + wide] = jnp.where(slot == local_id, piece, 0.0).astype(jnp.bfloat16)
+    for copy in loads[2:]:
+        copy.wait()
+    delta_q = jnp.dot(spread[...], bq[...], preferred_element_type=jnp.float32)
+    wider = shrunk.astype(jnp.float32)
+    shrunk_kv = jnp.where(
+        tensor < size // 2, wider[:, rank : 2 * rank], wider[:, 2 * rank : 3 * rank]
+    ).astype(jnp.bfloat16)
+    delta_kv = jnp.zeros((every, kvcols), jnp.float32)
+    for at in range(0, bkv.shape[0], wide):
+        product = lax.dot_general(
+            shrunk_kv, bkv[at : at + wide, :], (((1,), (1,)), ((), ())),
+            preferred_element_type=jnp.float32,
+        )
+        first = lax.broadcasted_iota(jnp.int32, product.shape, 1) + at - local_id * kvcols
+        product = jnp.where(jnp.logical_and(first >= 0, first < kvcols), product, 0.0)
+        lanes = product[:, :128]
+        for lane in range(128, wide, 128):
+            lanes = lanes + product[:, lane : lane + 128]
+        for lane in range(0, 128, kvcols):
+            delta_kv = delta_kv + lanes[:, lane : lane + kvcols]
+    rest = out_x.shape[2] - qcols - kvcols
+    out_x[...] = jnp.concatenate(
+        [delta_q, delta_kv, jnp.zeros((every, rest), jnp.float32)], 1
+    ).reshape(out_x.shape)
+    own = pl.ds(replica * size, size)
+    out_x[own] = out_x[own] + jnp.concatenate(
+        [base_q, base_kv, jnp.zeros((batch, rest), jnp.float32)], 1
+    ).reshape(size, rows, out_x.shape[2])
+    sent = []
+    for step, (other, peer) in enumerate(everyone):
+        copy = remote(out_x.at[other], out_in.at[me], send_o.at[step], recv_o.at[step], peer)
+        copy.start()
+        sent.append(copy)
+    out_in[me] = out_x[me]
     for step in range(depth - 1):
 
         @pl.when(jnp.logical_and(has_above, level - step >= 0))
@@ -297,9 +349,9 @@
 
     for at in range(depth):
         cross(at).wait_send()
-    for copy in copies:
-        copy.wait()
-    swap.wait()
+    for copy in sent:
+        copy.wait()
+    out_ref[...] = out_in[:size] + out_in[size:]
 
 
 def tail_kernel(
@@ -463,12 +515,6 @@
         out_ref[:, start + cols // 2 : start + cols] += extra[rows:]
 
 
-def fold_slices(rows, slices):
-    count, width = rows.shape
-    part = width // slices // 2
-    return rows.reshape(count, slices, 2, part).transpose(1, 0, 2, 3).reshape(slices, 2 * count, part)
-
-
 def shards(
     hidden,
     gain,
@@ -485,88 +531,69 @@
     down_weight_output,
     up_weight_output,
 ):
-    tensor_at = lax.axis_index("tensor")
     size = lax.axis_size("tensor")
-    replica_at = lax.axis_index("replica")
     own_rows, model_width = hidden.shape
     batch_rows = own_rows * size
     every_row = 2 * batch_rows
     hidden_wide = hidden.astype(jnp.float32)
     mean_square = jnp.mean(hidden_wide * hidden_wide, axis=-1, keepdims=True)
-    normalized_input = (hidden_wide * lax.rsqrt(mean_square + EPSILON) * gain).astype(jnp.bfloat16)
-
-    folded = fold_slices(normalized_input, size)
-    half = folded.shape[2]
+    normalized_input = hidden_wide * lax.rsqrt(mean_square + EPSILON) * gain
     id_tile = jnp.broadcast_to(request_adapter_index[:, None], (own_rows, 128))
     depth = size // 2
     dma = pltpu.SemaphoreType.DMA
     steps = max(depth - 1, 1)
-    gathered, other_features, id_tiles = call(
-        functools.partial(gather_kernel, size),
-        (
-            jax.ShapeDtypeStruct((size,) + folded.shape, jnp.bfloat16),
-            jax.ShapeDtypeStruct(folded.shape, jnp.bfloat16),
-            jax.ShapeDtypeStruct((2 * size, own_rows, 128), jnp.int32),
-        ),
-        [dma((2 * size - 1,)), dma((2 * size - 1,))] + [dma((steps,))] * 4 + [dma((depth,))] * 2
-        + [dma, dma],
-        0,
-        folded,
-        id_tile,
-    )
-    own_features = lax.dynamic_index_in_dim(gathered, tensor_at, 1, keepdims=False)
-
-    def unfold(blocks):
-        return (
-            blocks.reshape(size, own_rows, 2, half).reshape(batch_rows, 2 * half)
-        )
-
-    own_features, other_features = unfold(own_features), unfold(other_features)
-    features = jnp.where(
-        replica_at == 0,
-        jnp.concatenate([own_features, other_features], 0),
-        jnp.concatenate([other_features, own_features], 0),
-    )
-    full = (
-        gathered.reshape(size, size, own_rows, 2, half)
-        .transpose(0, 2, 1, 3, 4)
-        .reshape(batch_rows, model_width)
-    )
-    every_id = id_tiles[:, :, 0].reshape(every_row)
-    slots = down_weight_qkv.shape[1]
-    onehot = (
-        (every_id - replica_at * slots)[:, None] == jnp.arange(slots, dtype=jnp.int32)[None, :]
-    ).astype(jnp.float32)
-    reduced_input = reduce_and_gather(pick_down(features, down_weight_qkv, onehot), size, 1)
-    base = jnp.concatenate(
-        [
-            jnp.dot(full, query_weight, preferred_element_type=jnp.float32),
-            jnp.dot(full, key_value_weight, preferred_element_type=jnp.float32),
-        ],
-        1,
-    )
+    vmem, f32, bf16 = pltpu.VMEM, jnp.float32, jnp.bfloat16
+    double = 2 * own_rows
+    part_cols, slots, triple = down_weight_qkv.shape
     rank_size = up_weight_query.shape[0]
-    shrink_kv = jnp.where(
-        tensor_at < size // 2,
-        reduced_input[:, rank_size : 2 * rank_size],
-        reduced_input[:, 2 * rank_size :],
-    )
-    delta = jnp.concatenate(
-        [
-            pick_up(reduced_input[:, :rank_size], up_weight_query, onehot),
-            pick_up(shrink_kv, up_weight_key_value, onehot),
-        ],
-        1,
-    ).reshape(2, batch_rows, -1)
-    own = (jnp.arange(2) == replica_at)[:, None, None]
-    delta = delta + jnp.where(own, base[None], 0.0)
     query_cols = query_weight.shape[1]
     kv_cols = key_value_weight.shape[1]
     padded = -(-(query_cols + kv_cols) // 128) * 128
-    delta = jnp.pad(delta, ((0, 0), (0, 0), (0, padded - query_cols - kv_cols)))
-    arrived = exchange(delta.reshape(2 * size, own_rows, padded), size, 2)
-    arrived = arrived.reshape(2, size, own_rows, padded)
-    arrived = (arrived[0] + arrived[1]).astype(jnp.bfloat16).transpose(1, 0, 2)
+    red = -(-triple // 128) * 128
+    down_qkv = down_weight_qkv.transpose(1, 2, 0).reshape(slots * triple, part_cols)
+    up_q = up_weight_query.reshape(rank_size * slots, query_cols)
+    up_kv = up_weight_key_value.transpose(1, 2, 0).reshape(slots * kv_cols, rank_size)
+    kv_weight = key_value_weight.T
+    half = part_cols // 2
+    arrived, id_tiles = pl.pallas_call(
+        functools.partial(head_kernel, size, rank_size),
+        out_shape=(
+            jax.ShapeDtypeStruct((size, own_rows, padded), f32),
+            jax.ShapeDtypeStruct((2 * size, own_rows, 128), jnp.int32),
+        ),
+        in_specs=[pl.BlockSpec(memory_space=vmem)] * 2 + [pl.BlockSpec(memory_space=pl.ANY)] * 5,
+        out_specs=(pl.BlockSpec(memory_space=vmem), pl.BlockSpec(memory_space=vmem)),
+        scratch_shapes=[
+            vmem(down_qkv.shape, bf16),
+            vmem(query_weight.shape, bf16),
+            vmem(kv_weight.shape, bf16),
+            vmem(up_q.shape, bf16),
+            vmem(up_kv.shape, bf16),
+            vmem((size, double, half), bf16),
+            vmem((size, size, double, half), bf16),
+            vmem((2 * size, double, half), bf16),
+            vmem((every_row, part_cols), bf16),
+            vmem((every_row, 2 * triple), f32),
+            vmem((size, double, red), f32),
+            vmem((size, double, red), f32),
+            vmem((double, red), bf16),
+            vmem((size, double, red), bf16),
+            vmem((every_row, rank_size * slots), bf16),
+            vmem((2 * size, own_rows, padded), f32),
+            vmem((2 * size, own_rows, padded), f32),
+            dma((slots // 2,)),
+            dma((4,)),
+        ]
+        + [dma((2 * size - 1,))] * 4
+        + [dma((steps,))] * 4
+        + [dma((depth,))] * 2
+        + [dma((size - 1,))] * 4
+        + [dma((2 * size - 1,))] * 2,
+        compiler_params=pltpu.CompilerParams(
+            collective_id=0, has_side_effects=True, vmem_limit_bytes=VMEM_LIMIT
+        ),
+    )(normalized_input, id_tile, down_qkv, query_weight, kv_weight, up_q, up_kv)
+    arrived = arrived.astype(bf16).transpose(1, 0, 2)
     query_rows = arrived[:, :, :query_cols].reshape(own_rows, size * query_cols)
     kv_rows = arrived[:, :, query_cols : query_cols + kv_cols].reshape(own_rows, size * kv_cols)
     head_count = query_rows.shape[1] // HEAD_WIDTH

time: 113 us -> 93.9 us (0.83)
  matrix products: 15.4 us -> 0.66 us
  local copies, waits for them, and re-layouts: 10.1 us -> 5.55 us
    dot_general x5 -> x0, matrix products: 13.7 us -> none  [the longest x1 8.82 us: pick_down(): jnp.dot(left_rows, table.reshape(inner_dim, slots * columns), preferred_e...]
    reshape x5 -> x0, local copies, waits for them, and re-layouts: 5.4 us -> none  [the longest x2 3.61 us: shards(): gathered.reshape(size, size, own_rows, 2, half).transpose(0, 2, 1, 3, 4)]
    unnamed x15 -> x18, local copies, waits for them, and re-layouts: 2.6 us -> 4.64 us
    pallas_call x1, Pallas kernels: 38.1 us -> 40.1 us  [shards(): pl.pallas_call(functools.partial(tail_kernel, size, chunks, rank_out), ou...]
    pallas_call x3 -> x1, Pallas kernels: 44.7 us -> 43.5 us  [shards(): pl.pallas_call(functools.partial(head_kernel, size, rank_size), out_shape...]
where the time goes in v3:
time: 93.9 us; the launch traced here: 93.6 us
  Pallas kernels  83.6 us (89%)
  local copies, waits for them, and re-layouts  5.55 us (6%)
  other arithmetic  3.66 us (4%)
    pallas_call x1, Pallas kernels, shards(): pl.pallas_call(functools.partial(head_kernel, size, rank_size), out_shape...  43.5 us
    pallas_call x1, Pallas kernels, shards(): pl.pallas_call(functools.partial(tail_kernel, size, chunks, rank_out), ou...  40.1 us
    unnamed x18, local copies, waits for them, and re-layouts  4.64 us

profile of v3, /device:TPU:0, one launch (start us, length us, event | category | flops | bytes accessed | tf_op | source)
XLA Modules:
  0.0 93.6 jit_solution(17080929599917567657)
XLA Ops:
  0.0 1.1 %fusion.1 = f32[8]{0:T(128)S(1)} fusion(bf16[8,8192]{1,0:T(8,128)(2,1)} %param.14), kind=kLoop, calls=%fused_computation.4 | loop fusion | flops 196600 | bytes 131104 | tf_op jit(solution)/shard_map/reduce_sum | solution.py:539
  1.1 1.0 %fusion.2.x_ref = f32[8,8192]{1,0:T(8,128)S(1)} fusion(bf16[8,8192]{1,0:T(8,128)(2,1)} %param.14, f32[8192]{0:T(1024)} %param.15, f32[8]{0:T(128)S(1)} %add_rsqrt_fusion), kind=kLoop, calls=%fused_computation.5 | loop fusion | flops 196608 | bytes 426016 | tf_op jit(solution)/shard_map/mul | solution.py:540
  2.1 0.7 broadcast_in_dim.10.id_ref
  2.9 1.6 %copy-done.1 = bf16[8192,128]{1,0:T(8,128)(2,1)S(1)} copy-done((bf16[8192,128]{1,0:T(8,128)(2,1)S(1)}, bf16[8192,128]{1,0:T(8,128)(2,1)}, u32[]{:S(2)}) %copy-start.1) | copy-done | bytes 2097176
  4.5 1.0 %copy-done.3 = bf16[8192,32]{0,1:T(8,128)(2,1)S(1)} copy-done((bf16[8192,32]{0,1:T(8,128)(2,1)S(1)}, bf16[8192,32]{0,1:T(8,128)(2,1)}, u32[]{:S(2)}) %copy-start.3) | copy-done | bytes 524312
  5.5 1.0 %copy-done.4 = bf16[64,32,128]{2,1,0:T(8,128)(2,1)S(1)} copy-done((bf16[64,32,128]{2,1,0:T(8,128)(2,1)S(1)}, bf16[64,32,128]{2,1,0:T(8,128)(2,1)}, u32[]{:S(2)}) %copy-start.4) | copy-done | bytes 524312
  6.6 0.9 %copy-done.6 = bf16[64,32,32]{0,2,1:T(8,128)(2,1)S(1)} copy-done((bf16[64,32,32]{0,2,1:T(8,128)(2,1)S(1)}, bf16[64,32,32]{0,2,1:T(8,128)(2,1)}, u32[]{:S(2)}) %copy-start.6) | copy-done | bytes 131096
  7.5 43.5 %shard_map.136 = (f32[8,8,256]{2,1,0:T(8,128)S(1)}, s32[16,8,128]{2,1,0:T(8,128)S(1)}) custom-call(f32[8,8192]{1,0:T(8,128)S(1)} %fusion.2.x_ref, s32[8,128]{1,0:T(8,128)S(1)} %broadcast_in_dim.10.id_ref, bf16[6144,1024]{1,0:T(8,128)(2,1)} %bitcast.65, bf16[8192,128]{1,0:T(8,128)(2,1)S(1)} %copy-done.1, bf16[32,8192]{1,0:T(8,128)(2,1)S(1)} %bitcast.60, ...), custom_call_target="tpu_custom_call" | custom-call | tf_op jit(solution)/shard_map/pallas_call | solution.py:558
  51.1 0.1 multiply_cosine_fusion.1
  51.2 0.1 subtract_convert_fusion
  51.3 0.1 pad_maximum_fusion
  51.4 0.1 iota_compare_fusion
  51.5 0.3 fusion.29
  51.8 0.1 reshape.238
  51.9 0.1 fusion.28
  52.0 0.1 maximum_bitcast_fusion
  52.1 0.1 fusion.11
  52.2 0.2 fusion.7
  52.4 0.2 fusion.3
  52.7 0.1 copy.27
  52.7 0.1 fusion.8.x_ref
  52.8 0.0 copy-done.5
  52.8 40.1 %shard_map.137 = f32[8,8192]{1,0:T(8,128)S(1)} custom-call(s32[128,128]{1,0:T(8,128)S(1)} %bitcast.64, f32[8,8,128]{2,1,0:T(8,128)S(1)} %fusion.8.x_ref, bf16[2048,128]{1,0:T(8,128)(2,1)S(1)} %bitcast.62, bf16[128,8192]{1,0:T(8,128)(2,1)S(1)} %copy-done.2, bf16[2048,1024]{1,0:T(8,128)(2,1)} %bitcast.66), custom_call_target="tpu_custom_call" | custom-call | tf_op jit(solution)/shard_map/pallas_call | solution.py:622
  92.9 0.7 convert_element_type.70
  (24 shorter events, 0.1 us)
Async XLA Ops:
  0.0 51.5 %copy-start = (bf16[8,1,128,128]{3,2,1,0:T(8,128)(2,1)S(1)}, bf16[8,1,128,128]{3,2,1,0:T(8,128)(2,1)}, u32[]{:S(2)}) copy-start(bf16[8,1,128,128]{3,2,1,0:T(8,128)(2,1)} %param.18) | copy-start | bytes 786436
  2.9 1.6 %copy-start.1 = (bf16[8192,128]{1,0:T(8,128)(2,1)S(1)}, bf16[8192,128]{1,0:T(8,128)(2,1)}, u32[]{:S(2)}) copy-start(bf16[8192,128]{1,0:T(8,128)(2,1)} %wq_hbm.1) | copy-start | bytes 6291460
  4.5 1.0 %copy-start.3 = (bf16[8192,32]{0,1:T(8,128)(2,1)S(1)}, bf16[8192,32]{0,1:T(8,128)(2,1)}, u32[]{:S(2)}) copy-start(bf16[8192,32]{0,1:T(8,128)(2,1)} %param.21) | copy-start | bytes 1572868
  5.5 1.0 %copy-start.4 = (bf16[64,32,128]{2,1,0:T(8,128)(2,1)S(1)}, bf16[64,32,128]{2,1,0:T(8,128)(2,1)}, u32[]{:S(2)}) copy-start(bf16[64,32,128]{2,1,0:T(8,128)(2,1)} %param.24) | copy-start | bytes 1572868
  6.6 0.9 %copy-start.6 = (bf16[64,32,32]{0,2,1:T(8,128)(2,1)S(1)}, bf16[64,32,32]{0,2,1:T(8,128)(2,1)}, u32[]{:S(2)}) copy-start(bf16[64,32,32]{0,2,1:T(8,128)(2,1)} %param.25) | copy-start | bytes 393220
  7.5 43.6 %copy-start.8 = (s32[8]{0:T(128)S(1)}, s32[8]{0:T(128)}, u32[]{:S(2)}) copy-start(s32[8]{0:T(128)} %param.17) | copy-start | bytes 100
  7.5 44.9 %copy-start.7 = (bf16[8,1,128,128]{3,2,1,0:T(8,128)(2,1)S(1)}, bf16[8,1,128,128]{3,2,1,0:T(8,128)(2,1)}, u32[]{:S(2)}) copy-start(bf16[8,1,128,128]{3,2,1,0:T(8,128)(2,1)} %param.19) | copy-start | bytes 786436
  7.5 45.3 %copy-start.2 = (bf16[128,8192]{1,0:T(8,128)(2,1)S(1)}, bf16[128,8192]{1,0:T(8,128)(2,1)}, u32[]{:S(2)}) copy-start(bf16[128,8192]{1,0:T(8,128)(2,1)} %wo_hbm.1) | copy-start | bytes 6291460
  7.5 45.3 %copy-start.5 = (bf16[128,32,64]{0,2,1:T(8,128)(2,1)S(1)}, bf16[128,32,64]{0,2,1:T(8,128)(2,1)}, u32[]{:S(2)}) copy-start(bf16[128,32,64]{0,2,1:T(8,128)(2,1)} %param.26) | copy-start | bytes 1572868

commit v4 on v3

--- a/solution.py
+++ b/solution.py
@@ -615,7 +615,7 @@
     rank_out, _, out_cols = up_weight_output.shape
     down_table = down_weight_output.transpose(1, 2, 0).reshape(-1, head_cols)
     up_table = up_weight_output.reshape(rank_out * slots, out_cols)
-    chunks = 4
+    chunks = 2
     width = model_width // 2 // chunks
     double = 2 * own_rows
     vmem, f32, bf16 = pltpu.VMEM, jnp.float32, jnp.bfloat16

time: 93.9 us -> 90.7 us (0.966)
  Pallas kernels: 83.6 us -> 80.4 us
    pallas_call x1, Pallas kernels: 40.1 us -> 36.9 us  [shards(): pl.pallas_call(functools.partial(tail_kernel, size, chunks, rank_out), ou...]
where the time goes in v4:
time: 90.7 us; the launch traced here: 90.4 us
  Pallas kernels  80.4 us (89%)
  local copies, waits for them, and re-layouts  5.55 us (6%)
  other arithmetic  3.66 us (4%)
    pallas_call x1, Pallas kernels, shards(): pl.pallas_call(functools.partial(head_kernel, size, rank_size), out_shape...  43.5 us
    pallas_call x1, Pallas kernels, shards(): pl.pallas_call(functools.partial(tail_kernel, size, chunks, rank_out), ou...  36.9 us
    unnamed x18, local copies, waits for them, and re-layouts  4.64 us

profile of v4, /device:TPU:0, one launch (start us, length us, event | category | flops | bytes accessed | tf_op | source)
XLA Modules:
  0.0 90.4 jit_solution(5047015997500836179)
XLA Ops:
  0.0 1.1 %fusion.1 = f32[8]{0:T(128)S(1)} fusion(bf16[8,8192]{1,0:T(8,128)(2,1)} %param.14), kind=kLoop, calls=%fused_computation.4 | loop fusion | flops 196600 | bytes 131104 | tf_op jit(solution)/shard_map/reduce_sum | solution.py:539
  1.1 1.0 %fusion.2.x_ref = f32[8,8192]{1,0:T(8,128)S(1)} fusion(bf16[8,8192]{1,0:T(8,128)(2,1)} %param.14, f32[8192]{0:T(1024)} %param.15, f32[8]{0:T(128)S(1)} %add_rsqrt_fusion), kind=kLoop, calls=%fused_computation.5 | loop fusion | flops 196608 | bytes 426016 | tf_op jit(solution)/shard_map/mul | solution.py:540
  2.1 0.7 broadcast_in_dim.10.id_ref
  2.9 1.6 %copy-done.1 = bf16[8192,128]{1,0:T(8,128)(2,1)S(1)} copy-done((bf16[8192,128]{1,0:T(8,128)(2,1)S(1)}, bf16[8192,128]{1,0:T(8,128)(2,1)}, u32[]{:S(2)}) %copy-start.1) | copy-done | bytes 2097176
  4.5 1.0 %copy-done.3 = bf16[8192,32]{0,1:T(8,128)(2,1)S(1)} copy-done((bf16[8192,32]{0,1:T(8,128)(2,1)S(1)}, bf16[8192,32]{0,1:T(8,128)(2,1)}, u32[]{:S(2)}) %copy-start.3) | copy-done | bytes 524312
  5.5 1.0 %copy-done.4 = bf16[64,32,128]{2,1,0:T(8,128)(2,1)S(1)} copy-done((bf16[64,32,128]{2,1,0:T(8,128)(2,1)S(1)}, bf16[64,32,128]{2,1,0:T(8,128)(2,1)}, u32[]{:S(2)}) %copy-start.4) | copy-done | bytes 524312
  6.6 0.9 %copy-done.6 = bf16[64,32,32]{0,2,1:T(8,128)(2,1)S(1)} copy-done((bf16[64,32,32]{0,2,1:T(8,128)(2,1)S(1)}, bf16[64,32,32]{0,2,1:T(8,128)(2,1)}, u32[]{:S(2)}) %copy-start.6) | copy-done | bytes 131096
  7.5 43.5 %shard_map.136 = (f32[8,8,256]{2,1,0:T(8,128)S(1)}, s32[16,8,128]{2,1,0:T(8,128)S(1)}) custom-call(f32[8,8192]{1,0:T(8,128)S(1)} %fusion.2.x_ref, s32[8,128]{1,0:T(8,128)S(1)} %broadcast_in_dim.10.id_ref, bf16[6144,1024]{1,0:T(8,128)(2,1)} %bitcast.65, bf16[8192,128]{1,0:T(8,128)(2,1)S(1)} %copy-done.1, bf16[32,8192]{1,0:T(8,128)(2,1)S(1)} %bitcast.60, ...), custom_call_target="tpu_custom_call" | custom-call | tf_op jit(solution)/shard_map/pallas_call | solution.py:558
  51.1 0.1 multiply_cosine_fusion.1
  51.2 0.1 subtract_convert_fusion
  51.3 0.1 pad_maximum_fusion
  51.4 0.1 iota_compare_fusion
  51.5 0.3 fusion.29
  51.8 0.1 reshape.238
  51.9 0.1 fusion.28
  52.0 0.1 maximum_bitcast_fusion
  52.1 0.1 fusion.11
  52.2 0.2 fusion.7
  52.4 0.2 fusion.3
  52.7 0.1 copy.27
  52.7 0.1 fusion.8.x_ref
  52.8 0.0 copy-done.5
  52.8 36.9 %shard_map.137 = f32[8,8192]{1,0:T(8,128)S(1)} custom-call(s32[128,128]{1,0:T(8,128)S(1)} %bitcast.64, f32[8,8,128]{2,1,0:T(8,128)S(1)} %fusion.8.x_ref, bf16[2048,128]{1,0:T(8,128)(2,1)S(1)} %bitcast.62, bf16[128,8192]{1,0:T(8,128)(2,1)S(1)} %copy-done.2, bf16[2048,1024]{1,0:T(8,128)(2,1)} %bitcast.66), custom_call_target="tpu_custom_call" | custom-call | tf_op jit(solution)/shard_map/pallas_call | solution.py:622
  89.7 0.7 convert_element_type.70
  (24 shorter events, 0.1 us)
Async XLA Ops:
  0.0 51.5 %copy-start = (bf16[8,1,128,128]{3,2,1,0:T(8,128)(2,1)S(1)}, bf16[8,1,128,128]{3,2,1,0:T(8,128)(2,1)}, u32[]{:S(2)}) copy-start(bf16[8,1,128,128]{3,2,1,0:T(8,128)(2,1)} %param.18) | copy-start | bytes 786436
  2.9 1.6 %copy-start.1 = (bf16[8192,128]{1,0:T(8,128)(2,1)S(1)}, bf16[8192,128]{1,0:T(8,128)(2,1)}, u32[]{:S(2)}) copy-start(bf16[8192,128]{1,0:T(8,128)(2,1)} %wq_hbm.1) | copy-start | bytes 6291460
  4.5 1.0 %copy-start.3 = (bf16[8192,32]{0,1:T(8,128)(2,1)S(1)}, bf16[8192,32]{0,1:T(8,128)(2,1)}, u32[]{:S(2)}) copy-start(bf16[8192,32]{0,1:T(8,128)(2,1)} %param.21) | copy-start | bytes 1572868
  5.5 1.0 %copy-start.4 = (bf16[64,32,128]{2,1,0:T(8,128)(2,1)S(1)}, bf16[64,32,128]{2,1,0:T(8,128)(2,1)}, u32[]{:S(2)}) copy-start(bf16[64,32,128]{2,1,0:T(8,128)(2,1)} %param.24) | copy-start | bytes 1572868
  6.6 0.9 %copy-start.6 = (bf16[64,32,32]{0,2,1:T(8,128)(2,1)S(1)}, bf16[64,32,32]{0,2,1:T(8,128)(2,1)}, u32[]{:S(2)}) copy-start(bf16[64,32,32]{0,2,1:T(8,128)(2,1)} %param.25) | copy-start | bytes 393220
  7.5 43.6 %copy-start.8 = (s32[8]{0:T(128)S(1)}, s32[8]{0:T(128)}, u32[]{:S(2)}) copy-start(s32[8]{0:T(128)} %param.17) | copy-start | bytes 100
  7.5 44.9 %copy-start.7 = (bf16[8,1,128,128]{3,2,1,0:T(8,128)(2,1)S(1)}, bf16[8,1,128,128]{3,2,1,0:T(8,128)(2,1)}, u32[]{:S(2)}) copy-start(bf16[8,1,128,128]{3,2,1,0:T(8,128)(2,1)} %param.19) | copy-start | bytes 786436
  7.5 45.3 %copy-start.2 = (bf16[128,8192]{1,0:T(8,128)(2,1)S(1)}, bf16[128,8192]{1,0:T(8,128)(2,1)}, u32[]{:S(2)}) copy-start(bf16[128,8192]{1,0:T(8,128)(2,1)} %wo_hbm.1) | copy-start | bytes 6291460
  7.5 45.3 %copy-start.5 = (bf16[128,32,64]{0,2,1:T(8,128)(2,1)S(1)}, bf16[128,32,64]{0,2,1:T(8,128)(2,1)}, u32[]{:S(2)}) copy-start(bf16[128,32,64]{0,2,1:T(8,128)(2,1)} %param.26) | copy-start | bytes 1572868
